TPU v7x, 256 devices: a whole 4x4x8 slice. The times are simulated.
256 devices in a mesh: plane: 16 (over x, y), ax: 16 (over z, core).
Axes of the slice: x: 4, y: 4, z: 8, core: 2. Of those that a mesh axis runs over, the one named last changes fastest.
Arguments:
- source: float32 [1024, 256, 128], P('plane', 'ax'), may hold values from -6 to 6
- radial_basis: float32 [1024, 128, 128], P('plane'), may hold values from -0.5 to 0.5
- radial_weights: float32 [128], replicated, may hold values from 0.4 to 1.6
- mode_shifts: float32 [1024, 128], P('plane'), may hold values from 0.0001 to 0.03
Outputs:
- pressure: float32 [1024, 256, 128], P('plane', 'ax')
All inputs are finite; a program needn't handle non-finite values.
Results may differ from a plain program's by a relative error of at most 0.0003.
Values sent between devices are 32-bit elements; how exact they have to be, the bound alone decides.
No kernel may reach another device: no remote copies, remote signals or barrier semaphores. Data moves between devices by JAX's collectives and lax.ppermute only.
A program may use at most 64 MiB of HBM per device.

v0:
```python
import math

import jax
import jax.numpy as jnp
from jax import lax
from jax.sharding import PartitionSpec as P

axial_scale = 0.01


def basis_entry(mode_grid, angle_grid, length):
    middle = length // 2
    harmonic = jnp.where(mode_grid <= middle, mode_grid, mode_grid - middle)
    wrapped = harmonic * angle_grid % length
    radians = wrapped.astype(jnp.float32) * (2.0 * math.pi / length)
    factor = jnp.where(
        (mode_grid == 0) | (mode_grid == middle), math.sqrt(1.0 / length), math.sqrt(2.0 / length)
    )
    return jnp.where(mode_grid <= middle, jnp.cos(radians), jnp.sin(radians)) * factor


def tridiagonal_sweep(diagonal, rights):

    def forward(running, current):
        prior_factor, prior_carried = running
        denominator = diagonal + prior_factor
        multiplier = -1.0 / denominator
        carried = (current + prior_carried) / denominator
        return ((multiplier, carried), (multiplier, carried))

    zeroed = jnp.zeros_like(rights[0])
    finished, (factors, carries) = lax.scan(forward, (zeroed, zeroed), rights)

    def backward(following, entries):
        multiplier, carried = entries
        result = carried - multiplier * following
        return (result, result)

    finished, solved = lax.scan(backward, zeroed, (factors, carries), reverse=True)
    return solved


def join_segments(lower, upper):
    denominator = 1.0 - lower[5] * upper[1]
    joint_base = (lower[3] + lower[5] * upper[0]) / denominator
    joint_left = lower[4] / denominator
    joint_right = lower[5] * upper[2] / denominator
    cross_base = upper[0] + upper[1] * joint_base
    cross_left = upper[1] * joint_left
    cross_right = upper[2] + upper[1] * joint_right
    return (
        lower[0] + lower[2] * cross_base,
        lower[1] + lower[2] * cross_left,
        lower[2] * cross_right,
        upper[3] + upper[4] * joint_base,
        upper[4] * joint_left,
        upper[5] + upper[4] * joint_right,
    )


def body(source, radial_basis, radial_weights, mode_shifts):
    plane_count = lax.axis_size("plane")
    local_t, depth_cells, radius_count = source.shape
    total_t = local_t * plane_count
    angle_list = jnp.arange(total_t, dtype=jnp.int32)
    fourier = basis_entry(angle_list[:, None], angle_list[None, :], total_t)
    piece = lax.all_to_all(source, "plane", split_axis=2, concat_axis=0, tiled=True)
    flat_piece = piece.reshape(total_t, -1)
    product = jnp.dot(
        fourier, flat_piece, precision=lax.Precision.HIGHEST, preferred_element_type=jnp.float32
    )
    spectral = product.reshape(piece.shape)
    modal = lax.all_to_all(spectral, "plane", split_axis=0, concat_axis=2, tiled=True)
    spectra = jnp.einsum(
        "kzr,krj->zkj", modal * radial_weights, radial_basis, precision=lax.Precision.HIGHEST
    )
    positions = jnp.arange(depth_cells, dtype=jnp.int32)[:, None, None]
    head_mark = jnp.broadcast_to((positions == 0).astype(jnp.float32), spectra.shape)
    tail_mark = jnp.broadcast_to((positions == depth_cells - 1).astype(jnp.float32), spectra.shape)
    rights = jnp.stack([spectra * axial_scale, head_mark, tail_mark], axis=1)
    solved = tridiagonal_sweep((2.0 + mode_shifts)[None], rights)
    particular = solved[:, 0]
    left_response = solved[:, 1]
    right_response = solved[:, 2]
    segment = (
        particular[0],
        left_response[0],
        right_response[0],
        particular[-1],
        left_response[-1],
        right_response[-1],
    )
    zero_plane = jnp.zeros_like(particular[0])
    one_plane = jnp.ones_like(particular[0])
    identity = (zero_plane, zero_plane, one_plane, zero_plane, one_plane, zero_plane)
    stacked = jnp.stack(segment)[None]
    everyone = lax.all_gather(stacked, "ax", axis=0, tiled=True)

    def ascend(running, entry):
        members = tuple((entry[position] for position in range(6)))
        return (join_segments(running, members), running)

    def descend(running, entry):
        members = tuple((entry[position] for position in range(6)))
        return (join_segments(members, running), running)

    finished, prefixes = lax.scan(ascend, identity, everyone)
    finished, suffixes = lax.scan(descend, identity, everyone, reverse=True)
    axial_index = lax.axis_index("ax")
    from_lower = tuple(
        (lax.dynamic_index_in_dim(member, axial_index, 0, keepdims=False) for member in prefixes)
    )
    from_upper = tuple(
        (lax.dynamic_index_in_dim(member, axial_index, 0, keepdims=False) for member in suffixes)
    )
    below_base = from_lower[3]
    below_slope = from_lower[5]
    above_base = from_upper[0]
    above_slope = from_upper[1]
    head_known = segment[0] + segment[1] * below_base + segment[2] * above_base
    tail_known = segment[3] + segment[4] * below_base + segment[5] * above_base
    head_self = 1.0 - segment[1] * below_slope
    head_cross = segment[2] * above_slope
    tail_cross = segment[4] * below_slope
    tail_self = 1.0 - segment[5] * above_slope
    determinant = head_self * tail_self - head_cross * tail_cross
    head_value = (head_known * tail_self + head_cross * tail_known) / determinant
    tail_value = (head_self * tail_known + tail_cross * head_known) / determinant
    lower_value = below_base + below_slope * head_value
    upper_value = above_base + above_slope * tail_value
    axial = particular + left_response * lower_value + right_response * upper_value
    radial_field = jnp.einsum("zkj,krj->kzr", axial, radial_basis, precision=lax.Precision.HIGHEST)
    piece = lax.all_to_all(radial_field, "plane", split_axis=2, concat_axis=0, tiled=True)
    flat_piece = piece.reshape(total_t, -1)
    product = jnp.dot(
        fourier.T, flat_piece, precision=lax.Precision.HIGHEST, preferred_element_type=jnp.float32
    )
    spatial = product.reshape(piece.shape)
    pressure = lax.all_to_all(spatial, "plane", split_axis=0, concat_axis=2, tiled=True)
    return pressure


def solution(mesh):
    placed = (P("plane", "ax", None), P("plane", None, None), P(), P("plane", None))
    return jax.shard_map(
        body, mesh=mesh, in_specs=placed, out_specs=P("plane", "ax", None), check_vma=False
    )
```

profile of v0, /device:TPU:8, one launch (start us, length us, event | category | flops | bytes accessed | tf_op | source)
XLA Modules:
  0.0 296.4 jit_solution(996433478246644329)
XLA Ops:
  6.5 1.6 copy.43
  8.1 1.4 reshape.108
  9.6 7.4 %all-to-all-start = ((f32[16,1,8192]{2,1,0:T(1,128)}), f32[16,1,8192]{2,1,0:T(1,128)S(1)}, u32[]{:S(2)}, u32[]{:S(2)}) async-start(f32[16,1,8192]{2,1,0:T(1,128)} %reshape.108), calls=%async_computation | async-start | bytes 1048576 | tf_op jit(solution)/shard_map/all_to_all | solution.py:67
  17.0 19.2 %fusion.70 = f32[1024,1024,1]{1,0,2:T(8,128)} fusion(f32[1024]{0:T(1024)S(1)} %fusion.49, s32[1024]{0:T(1024)S(1)} %add_select_fusion.1, pred[1024]{0:T(1024)(128)(4,1)S(1)} %iota_compare_fusion.2), kind=kLoop, calls=%fused_computation.57.clone.1 | loop fusion | flops 16777216 | bytes 4203520 | tf_op jit(solution)/shard_map/dot_general | solution.py:69
  36.7 1.8 reduce
  39.9 6.8 %fusion.29 = f32[1024,16,8]{0,1,2:T(8,128)S(1)} fusion(f32[16,8,1024]{2,1,0:T(8,128)S(1)} %bitcast.290, f32[1024,1024,1]{1,0,2:T(8,128)} %fusion.70), kind=kOutput, calls=%fused_computation.56 | convolution fusion | flops 1610612736 | bytes 5242880 | tf_op jit(solution)/shard_map/dot_general | solution.py:69
  46.6 2.6 copy.47
  49.3 4.2 %reshape.110 = f32[16,1,8192]{2,1,0:T(1,128)} reshape(f32[1024,8,16]{2,1,0:T(8,128)} %bitcast.282) | data formatting | bytes 1048576
  53.5 7.2 %all-to-all-start.1 = ((f32[16,1,8192]{2,1,0:T(1,128)}), f32[16,1,8192]{2,1,0:T(1,128)S(1)}, u32[]{:S(2)}, u32[]{:S(2)}) async-start(f32[16,1,8192]{2,1,0:T(1,128)} %reshape.110), calls=%async_computation.1 | async-start | bytes 1048576 | tf_op jit(solution)/shard_map/all_to_all | solution.py:73
  61.6 8.7 %all-to-all-done.1 = f32[16,1,8192]{2,1,0:T(1,128)S(1)} async-done(((f32[16,1,8192]{2,1,0:T(1,128)}), f32[16,1,8192]{2,1,0:T(1,128)S(1)}, u32[]{:S(2)}, u32[]{:S(2)}) %all-to-all-start.1) | async-done | bytes 524320 | tf_op jit(solution)/shard_map/all_to_all | solution.py:73
  70.3 1.8 reduce.1
  72.1 2.8 reshape.111
  74.9 3.2 %copy.48 = f32[16,64,16,8]{1,3,0,2:T(8,128)S(1)} copy(f32[16,64,16,8]{2,3,1,0:T(8,128)} %bitcast.280) | data formatting | bytes 1048576 | tf_op jit(solution)/shard_map/all_to_all | solution.py:73
  78.7 5.3 %fusion.34 = f32[16,1,64,128]{3,0,2,1:T(8,128)S(1)} fusion(f32[64,16,128]{2,1,0:T(8,128)S(1)} %copy.49, f32[64,128,128]{2,1,0:T(8,128)} %param.13), kind=kOutput, calls=%fused_computation.64 | convolution fusion | flops 201457664 | bytes 5242880 | tf_op jit(solution)/shard_map/kzr,krj->zkj/dot_general | solution.py:74
  84.5 1.3 broadcast.95.clone.1
  85.8 24.6 %while.72 = (s32[]{:T(128)}, f32[3,64,128]{2,1,0:T(8,128)S(1)}, f32[3,64,128]{2,1,0:T(8,128)S(1)}, f32[16,3,64,128]{3,2,1,0:T(8,128)S(1)}, f32[16,3,64,128]{3,2,...) while((s32[]{:T(128)}, f32[3,64,128]{2,1,0:T(8,128)S(1)}, ...), condition=%wide.region_1.2_spmd.clone, body=%wide.region_0.1_spmd.clone.sunk | while | flops 147459 | bytes 918123 | solution.py:32
  85.9 1.5 bitcast_dynamic-update-slice_fusion.19
  87.4 1.5 bitcast_dynamic-update-slice_fusion.19
  89.0 1.5 bitcast_dynamic-update-slice_fusion.19
  90.5 1.4 bitcast_dynamic-update-slice_fusion.19
  92.1 1.5 bitcast_dynamic-update-slice_fusion.19
  93.6 1.5 bitcast_dynamic-update-slice_fusion.19
  95.1 1.5 bitcast_dynamic-update-slice_fusion.19
  96.7 1.5 bitcast_dynamic-update-slice_fusion.19
  98.2 1.5 bitcast_dynamic-update-slice_fusion.19
  99.7 1.5 bitcast_dynamic-update-slice_fusion.19
  101.3 1.5 bitcast_dynamic-update-slice_fusion.19
  102.8 1.5 bitcast_dynamic-update-slice_fusion.19
  104.4 1.5 bitcast_dynamic-update-slice_fusion.19
  105.9 1.5 bitcast_dynamic-update-slice_fusion.19
  107.4 1.5 bitcast_dynamic-update-slice_fusion.19
  109.0 1.5 bitcast_dynamic-update-slice_fusion.19
  110.6 15.8 %while.73 = (s32[]{:T(128)}, f32[3,64,128]{2,1,0:T(8,128)S(1)}, f32[16,3,64,128]{3,2,1,0:T(8,128)S(1)}, f32[16,3,64,128]{3,2,1,0:T(8,128)}, f32[16,3,64,128]{3,2...) while((s32[]{:T(128)}, f32[3,64,128]{2,1,0:T(8,128)S(1)}, f32[16,3,64,128]{3,2,1,0:T(8,128)S(1)}, ...), condition=%wide.region_3.4_spmd.clone, body=%wide.region_2.3_spmd.clone.sunk | while | flops 73732 | bytes 491631 | solution.py:39
  110.6 1.0 bitcast_dynamic-update-slice_fusion.20
  111.6 1.0 bitcast_dynamic-update-slice_fusion.20
  112.6 1.0 bitcast_dynamic-update-slice_fusion.20
  113.6 1.0 bitcast_dynamic-update-slice_fusion.20
  114.6 1.0 bitcast_dynamic-update-slice_fusion.20
  115.5 1.0 bitcast_dynamic-update-slice_fusion.20
  116.5 1.0 bitcast_dynamic-update-slice_fusion.20
  117.5 1.0 bitcast_dynamic-update-slice_fusion.20
  118.5 1.0 bitcast_dynamic-update-slice_fusion.20
  119.5 1.0 bitcast_dynamic-update-slice_fusion.20
  120.5 1.0 bitcast_dynamic-update-slice_fusion.20
  121.5 1.0 bitcast_dynamic-update-slice_fusion.20
  122.4 1.0 bitcast_dynamic-update-slice_fusion.20
  123.4 1.0 bitcast_dynamic-update-slice_fusion.20
  124.4 1.0 bitcast_dynamic-update-slice_fusion.20
  125.4 1.0 bitcast_dynamic-update-slice_fusion.20
  127.2 41.4 %all-gather.3.cloned.1.call-done = f32[96,64,128]{2,1,0:T(8,128)} async-done(((f32[6,64,128]{2,1,0:T(8,128)}), f32[96,64,128]{2,1,0:T(8,128)}) %all-gather.3.cloned.1.call-update) | async-done | bytes 3145744 | tf_op jit(solution)/shard_map/all_gather | solution.py:97
  168.7 14.7 %while.71 = (s32[]{:T(128)}, f32[64,128]{1,0:T(8,128)S(1)}, f32[64,128]{1,0:T(8,128)S(1)}, f32[16,64,128]{2,1,0:T(8,128)S(1)}, f32[16,64,128]{2,1,0:T(8,128)S(1)...) while((s32[]{:T(128)}, f32[64,128]{1,0:T(8,128)S(1)}, ...), condition=%wide.region_7.8_spmd, body=%wide.region_6.7_spmd.sunk | while | flops 106504 | bytes 458985 | solution.py:108
  175.2 0.9 fusion.75
  184.3 24.1 %while.70 = (s32[]{:T(128)}, f32[64,128]{1,0:T(8,128)S(1)}, f32[64,128]{1,0:T(8,128)S(1)}, f32[16,64,128]{2,1,0:T(8,128)}, f32[16,64,128]{2,1,0:T(8,128)S(1)}, /...) while((s32[]{:T(128)}, f32[64,128]{1,0:T(8,128)S(1)}, ...), condition=%wide.region_5.6_spmd, body=%wide.region_4.5_spmd.sunk | while | flops 90119 | bytes 459473 | solution.py:107
  209.4 8.3 %fusion.39 = f32[64,16,128]{2,1,0:T(8,128)S(1)} fusion(f32[64,128,128]{2,1,0:T(8,128)} %param.13, f32[16,64,128]{2,1,0:T(8,128)S(1)} %fusion.36), kind=kOutput, calls=%fused_computation.73 | convolution fusion | flops 201326592 | bytes 5242880 | tf_op jit(solution)/shard_map/zkj,krj->kzr/dot_general | solution.py:132
  219.0 17.6 %all_to_all.66 = f32[16,1,8192]{2,1,0:T(1,128)S(1)} all-to-all(f32[16,1,8192]{2,1,0:T(1,128)S(1)} %reshape.112), channel_id=1, replica_groups=mesh['plane'=16,'ax'=16] {'plane'}, dimensions={0} | all-to-all | bytes 1048576 | tf_op jit(solution)/shard_map/all_to_all | solution.py:133
  236.6 1.8 reduce.2
  239.8 20.6 %fusion.27 = f32[1024,16,8]{0,1,2:T(8,128)S(1)} fusion(f32[1024]{0:T(1024)S(1)} %fusion.49, s32[1024]{0:T(1024)S(1)} %add_select_fusion.1, pred[1024]{0:T(1024)(128)(4,1)S(1)} %iota_compare_fusion.2, f32[16,8,1024]{2,1,0:T(8,128)S(1)} %bitcast.293), kind=kOutput, calls=%fused_computation.54 | convolution fusion | flops 1627389952 | bytes 1057792 | tf_op jit(solution)/shard_map/dot_general | solution.py:135
  260.4 2.6 copy.58
  263.1 3.5 %reshape.114 = f32[16,1,8192]{2,1,0:T(1,128)S(1)} reshape(f32[1024,8,16]{2,1,0:T(8,128)} %bitcast.283) | data formatting | bytes 1048576
  266.6 14.0 %all_to_all.67 = f32[16,1,8192]{2,1,0:T(1,128)S(1)} all-to-all(f32[16,1,8192]{2,1,0:T(1,128)S(1)} %reshape.114), channel_id=1, replica_groups=mesh['plane'=16,'ax'=16] {'plane'}, dimensions={0} | all-to-all | bytes 1048576 | tf_op jit(solution)/shard_map/all_to_all | solution.py:139
  280.6 1.8 reduce.3
  282.4 2.8 reshape.115
  285.2 3.2 %copy.59 = f32[16,64,16,8]{1,3,0,2:T(8,128)S(1)} copy(f32[16,64,16,8]{2,3,1,0:T(8,128)} %bitcast.281) | data formatting | bytes 1048576 | tf_op jit(solution)/shard_map/all_to_all | solution.py:139
  288.4 1.1 copy.60
  (130 shorter events, 47.6 us)
Async XLA Ops:
  9.6 26.6 %all-to-all-start = ((f32[16,1,8192]{2,1,0:T(1,128)}), f32[16,1,8192]{2,1,0:T(1,128)S(1)}, u32[]{:S(2)}, u32[]{:S(2)}) async-start(f32[16,1,8192]{2,1,0:T(1,128)} %reshape.108), calls=%async_computation | async-start | bytes 1048576 | tf_op jit(solution)/shard_map/all_to_all | solution.py:67
  46.6 14.3 %copy-start.1 = (f32[64,128]{1,0:T(8,128)S(1)}, f32[64,128]{1,0:T(8,128)}, u32[]{:S(2)}) copy-start(f32[64,128]{1,0:T(8,128)} %param.15) | copy-start | bytes 98308
  53.5 16.8 %all-to-all-start.1 = ((f32[16,1,8192]{2,1,0:T(1,128)}), f32[16,1,8192]{2,1,0:T(1,128)S(1)}, u32[]{:S(2)}, u32[]{:S(2)}) async-start(f32[16,1,8192]{2,1,0:T(1,128)} %reshape.110), calls=%async_computation.1 | async-start | bytes 1048576 | tf_op jit(solution)/shard_map/all_to_all | solution.py:73
  60.7 107.9 %all-gather.3.cloned.1.call-start = ((), (), s32[]{:S(2)}) async-start(), calls=%async_computation.4 | async-start | bytes 3342336 | tf_op jit(solution)/shard_map/all_gather | solution.py:97
  72.1 6.0 %copy-start.2 = (f32[128]{0:T(128)S(1)}, f32[128]{0:T(128)}, u32[]{:S(2)}) copy-start(f32[128]{0:T(128)} %param.14) | copy-start | bytes 1540
  126.5 0.7 copy-start
Sparse Core Ops, SparseCore 0:
  127.3 41.2 all-gather.2
where the time goes:
time: 301 us; the launch traced here: 296 us
  other arithmetic  95 us (32%)
  waiting for transfers between devices  50.1 us (17%)
  local copies, waits for them, and re-layouts  48.8 us (16%)
  matrix products  41 us (14%)
  blocking collectives  31.6 us (10%)
  starting transfers between devices  14.8 us (5%)
  between operations  13.8 us (5%)
    all_gather x1, waiting for transfers between devices, body(): everyone = lax.all_gather(stacked, 'ax', axis=0, tiled=True)  41.4 us
    dynamic_update_slice x32, other arithmetic, tridiagonal_sweep(): finished, (factors, carries) = lax.scan(forward, (zeroed, zeroed), rights)  38.8 us
    dot_general x1, matrix products, body(): jnp.dot(fourier.T, flat_piece, precision=lax.Precision.HIGHEST, preferred...  20.6 us
    dot_general x1, other arithmetic, body(): jnp.dot(fourier, flat_piece, precision=lax.Precision.HIGHEST, preferred_e...  19.2 us
    unnamed x20, local copies, waits for them, and re-layouts  18.5 us
    all_to_all x1, blocking collectives, body(): lax.all_to_all(radial_field, 'plane', split_axis=2, concat_axis=0, tiled=...  17.6 us
    add x16, other arithmetic, join_segments(): lower[1] + lower[2] * cross_left  14.1 us
    all_to_all x1, blocking collectives, body(): lax.all_to_all(spatial, 'plane', split_axis=0, concat_axis=2, tiled=True)  14 us
  transfers between devices with their start and end apart: 3, of which 2 were waited for; matrix products, arithmetic and copies ran while one was open for 7% of the time, Pallas kernels for 0%

commit v1 on v0

v1 whole, which is shorter than its diff:
```python
import functools
import math

import jax
import jax.numpy as jnp
import ml_dtypes
import numpy as np
from jax import lax
from jax.experimental import pallas as pl
from jax.experimental.pallas import tpu as pltpu
from jax.sharding import PartitionSpec as P

axial_scale = 0.01
merge = 2
bf16 = jnp.bfloat16
f32 = jnp.float32


def mode_order(total, planes, share):
    local = total // planes
    size = local // share
    share_at, plane_at, parity, half = np.meshgrid(
        np.arange(share), np.arange(planes), np.arange(2), np.arange(size // 2), indexing="ij"
    )
    return plane_at * local + share_at * size + 2 * half + parity


def fourier_halves(total, planes, share):
    order = mode_order(total, planes, share).transpose(2, 0, 1, 3).reshape(2, total // 2)
    angles = np.arange(total // 2)
    middle = total // 2
    harmonic = np.where(order <= middle, order, order - middle)
    radians = (harmonic[:, :, None] * angles % total) * (2.0 * math.pi / total)
    factor = np.where((order == 0) | (order == middle), math.sqrt(1.0 / total), math.sqrt(2.0 / total))
    waves = np.where((order <= middle)[:, :, None], np.cos(radians), np.sin(radians))
    return (waves * factor[:, :, None]).astype(np.float32)


def split_table(table, parts):
    rest = table.astype(np.float32)
    pieces = []
    for _ in range(parts):
        piece = rest.astype(ml_dtypes.bfloat16)
        pieces.append(piece)
        rest = rest - piece.astype(np.float32)
    return np.stack(pieces)


def split2(value):
    high = value.astype(bf16)
    return high, (value - high.astype(f32)).astype(bf16)


def split3(value):
    high = value.astype(bf16)
    rest = value - high.astype(f32)
    middle = rest.astype(bf16)
    return high, middle, (rest - middle.astype(f32)).astype(bf16)


def mul(left, right):
    return jnp.dot(left, right, preferred_element_type=f32)


def mul_t(left, right):
    return lax.dot_general(left, right, (((1,), (1,)), ((), ())), preferred_element_type=f32)


def forward_kernel(table_ref, x_ref, out_ref):
    half_t = x_ref.shape[0] // 2
    width = x_ref.shape[1]
    blocks, size, _ = out_ref.shape
    low, high = x_ref[:half_t], x_ref[half_t:]
    for parity in range(2):
        folded = low + high if parity == 0 else low - high
        a, b, c = split3(folded)
        pair = jnp.concatenate([a, b], axis=1)
        first = mul(table_ref[0, parity], pair)
        second = mul(table_ref[1, parity], pair)
        third = mul(table_ref[0, parity], c) + mul(table_ref[2, parity], a)
        result = first[:, :width] + (
            (first[:, width:] + second[:, :width]) + (third + second[:, width:])
        )
        out_ref[:, parity * (size // 2) : (parity + 1) * (size // 2), :] = result.reshape(
            blocks, size // 2, width
        )


def backward_kernel(table_ref, x_ref, out_ref):
    blocks, size, width = x_ref.shape
    sums = []
    for parity in range(2):
        part = x_ref[:, parity * (size // 2) : (parity + 1) * (size // 2), :].reshape(-1, width)
        a, b = split2(part)
        pair = jnp.concatenate([a, b], axis=1)
        first = mul(table_ref[0, parity], pair)
        sums.append(first[:, :width] + (first[:, width:] + mul(table_ref[1, parity], a)))
    half_t = out_ref.shape[0] // 2
    out_ref[:half_t] = sums[0] + sums[1]
    out_ref[half_t:] = sums[0] - sums[1]


def modal_kernel(x_ref, basis_ref, weights_ref, decay_ref, f_ref, carry_ref):
    depth, size, _ = x_ref.shape
    weights = weights_ref[...]
    for place in range(size):
        parity, half = divmod(place, size // 2)
        a, b, c = split3(x_ref[:, place, :] * weights)
        ra, rb, rc = split3(basis_ref[2 * half + parity])
        small = mul(a, rc) + mul(c, ra) + mul(b, rb)
        f_ref[:, place, :] = mul(a, ra) + ((mul(a, rb) + mul(b, ra)) + small)
    decay = decay_ref[...]
    up = f_ref[0]
    down = f_ref[depth - 1]
    for step in range(1, depth):
        up = up * decay + f_ref[step]
        down = down * decay + f_ref[depth - 1 - step]
    carry_ref[0] = up
    carry_ref[1] = down


def solve_kernel(f_ref, basis_ref, decay_ref, gain_ref, start_ref, out_ref, y_ref):
    depth, size, _ = f_ref.shape
    decay = decay_ref[...]
    gain = gain_ref[...]
    up = start_ref[0]
    for step in range(depth):
        up = up * decay
        y_ref[step] = up
        up = up + f_ref[step]
    down = start_ref[1]
    for step in range(depth - 1, -1, -1):
        down = down * decay + f_ref[step]
        y_ref[step] = (y_ref[step] + down) * gain
    for place in range(size):
        parity, half = divmod(place, size // 2)
        a, b = split2(y_ref[:, place, :])
        ra, rb = split2(basis_ref[2 * half + parity])
        out_ref[:, place, :] = mul_t(a, ra) + (mul_t(a, rb) + mul_t(b, ra))


def whole(memory_space=pltpu.VMEM):
    return pl.BlockSpec(memory_space=memory_space)


def body(source, radial_basis, radial_weights, mode_shifts):
    planes = lax.axis_size("plane")
    blocks = lax.axis_size("ax")
    local_t, depth_cells, radius_count = source.shape
    total_t = local_t * planes
    axial_cells = depth_cells * blocks
    size = local_t // merge
    span = depth_cells * merge
    table = fourier_halves(total_t, planes, merge)
    forward_table = jnp.asarray(split_table(table, 3))
    backward_table = jnp.asarray(split_table(table.transpose(0, 2, 1), 2))
    teams = [
        [plane * blocks + first + share for share in range(merge) for plane in range(planes)]
        for first in range(0, blocks, merge)
    ]

    axial_index = lax.axis_index("ax")
    share = axial_index % merge
    block = axial_index // merge
    shifts = lax.dynamic_slice_in_dim(mode_shifts, share * size, size, 0)
    shifts = shifts.reshape(size // 2, 2, radius_count).transpose(1, 0, 2).reshape(size, radius_count)
    basis = lax.dynamic_slice_in_dim(radial_basis, share * size, size, 0)
    rounded = lax.reduce_precision(2.0 + shifts, 8, 23) - 2.0
    rise = 0.5 * jnp.sqrt(rounded)
    cosh_half = jnp.sqrt(1.0 + rise * rise)
    root = cosh_half - rise
    decay = root * root
    gain = axial_scale / (4.0 * rise * cosh_half)

    def power(base, count):
        result = None
        while count:
            if count & 1:
                result = base if result is None else result * base
            base = base * base
            count >>= 1
        return result

    def device_power(base, count, limit):
        result = jnp.ones_like(base)
        bit = 1
        while bit < limit:
            result = jnp.where((count & bit) != 0, result * base, result)
            base = base * base
            bit *= 2
        return result

    teams_along = blocks // merge
    span_decay = power(decay, span)
    to_first = device_power(span_decay, block, teams_along)
    to_last = device_power(span_decay, teams_along - 1 - block, teams_along)
    whole_decay = power(decay, axial_cells + 1)
    closing = decay / (1.0 - whole_decay * whole_decay)

    piece = lax.all_to_all(source.transpose(1, 0, 2), "plane", 0, 0, tiled=True)
    spectral = pl.pallas_call(
        forward_kernel,
        out_shape=jax.ShapeDtypeStruct((planes * merge, size, radius_count), f32),
        in_specs=[whole(), whole()],
        out_specs=whole(),
        name="fourier_forward",
    )(forward_table, piece.reshape(total_t, radius_count))
    modal = lax.all_to_all(
        spectral, ("plane", "ax"), 0, 0, tiled=True, axis_index_groups=teams
    )
    spectra, carries = pl.pallas_call(
        modal_kernel,
        out_shape=(
            jax.ShapeDtypeStruct((span, size, radius_count), f32),
            jax.ShapeDtypeStruct((2, size, radius_count), f32),
        ),
        in_specs=[whole()] * 4,
        out_specs=(whole(), whole()),
        name="radial_forward",
    )(modal, basis, radial_weights.reshape(1, radius_count), decay)

    up, down = carries[0], carries[1]
    from_below = jnp.zeros_like(up)
    from_above = jnp.zeros_like(up)
    reach = 1
    reach_decay = span_decay
    while reach < teams_along:
        stride = reach * merge
        swap = [(index, index ^ stride) for index in range(blocks)]
        other = lax.ppermute(jnp.stack([up, down]), "ax", swap)
        above = (block & reach) != 0
        offset = block & (reach - 1)
        near_below = device_power(span_decay, offset, reach)
        near_above = device_power(span_decay, reach - 1 - offset, reach)
        from_below = jnp.where(above, from_below + near_below * other[0], from_below)
        from_above = jnp.where(above, from_above, from_above + near_above * other[1])
        up = jnp.where(above, up + reach_decay * other[0], other[0] + reach_decay * up)
        down = jnp.where(above, other[1] + reach_decay * down, down + reach_decay * other[1])
        reach *= 2
        reach_decay = reach_decay * reach_decay
    start_below = from_below - closing * (down - whole_decay * up) * to_first
    start_above = from_above - closing * (up - whole_decay * down) * to_last

    radial_field = pl.pallas_call(
        solve_kernel,
        out_shape=jax.ShapeDtypeStruct((span, size, radius_count), f32),
        in_specs=[whole()] * 5,
        out_specs=whole(),
        scratch_shapes=[pltpu.VMEM((span, size, radius_count), f32)],
        name="solve_and_radial_back",
    )(spectra, basis, decay, gain, jnp.stack([start_below, start_above]))
    collected = lax.all_to_all(
        radial_field, ("plane", "ax"), 0, 0, tiled=True, axis_index_groups=teams
    )
    spatial = pl.pallas_call(
        backward_kernel,
        out_shape=jax.ShapeDtypeStruct((total_t, radius_count), f32),
        in_specs=[whole(), whole()],
        out_specs=whole(),
        name="fourier_backward",
    )(backward_table, collected)
    pressure = lax.all_to_all(
        spatial.reshape(planes, local_t, radius_count), "plane", 0, 0, tiled=True
    )
    return pressure.transpose(1, 0, 2)


def solution(mesh):
    placed = (P("plane", "ax", None), P("plane", None, None), P(), P("plane", None))
    return jax.shard_map(
        body, mesh=mesh, in_specs=placed, out_specs=P("plane", "ax", None), check_vma=False
    )
```

time: 301 us -> 105 us (0.35); the launches traced: 296 us -> 104 us
  other arithmetic: 95 us -> 2.15 us
  local copies, waits for them, and re-layouts: 48.8 us -> 6.27 us
  matrix products: 41 us -> 0 us
  waiting for transfers between devices: 50.1 us -> 12.6 us
  blocking collectives: 31.6 us -> 49.3 us
  Pallas kernels: 0 us -> 16.5 us
  between operations: 13.8 us -> 0.12 us
    all_gather x1 -> x0, waiting for transfers between devices: 41.4 us -> none  [body(): everyone = lax.all_gather(stacked, 'ax', axis=0, tiled=True)]
    dot_general x4 -> x0, matrix products: 41 us -> none  [the longest x1 20.6 us: body(): jnp.dot(fourier.T, flat_piece, precision=lax.Precision.HIGHEST, preferred...]
    dynamic_update_slice x32 -> x0, other arithmetic: 38.8 us -> none  [tridiagonal_sweep(): finished, (factors, carries) = lax.scan(forward, (zeroed, zeroed), rights)]
    add x33 -> x0, other arithmetic: 28.1 us -> none  [the longest x16 14.1 us: join_segments(): lower[1] + lower[2] * cross_left]
    dot_general x1 -> x0, other arithmetic: 19.2 us -> none  [body(): jnp.dot(fourier, flat_piece, precision=lax.Precision.HIGHEST, preferred_e...]
    all_to_all x2 -> x3, blocking collectives: 31.6 us -> 49.3 us  [the longest x1 17.4 us: body(): piece = lax.all_to_all(source.transpose(1, 0, 2), 'plane', 0, 0, tiled=True)]
    pallas_call x0 -> x4, Pallas kernels: none -> 16.5 us  [the longest x1 4.86 us: body(): pl.pallas_call(solve_kernel, out_shape=jax.ShapeDtypeStruct((span, size,...]
    unnamed x20 -> x5, local copies, waits for them, and re-layouts: 18.5 us -> 2.01 us
  transfers between devices with their start and end apart: 3 -> 4, of which waited for: 2 -> 4; matrix products, arithmetic and copies ran while one was open for 7% -> 4% of each run, Pallas kernels for 0% -> 0%
where the time goes in v1:
time: 105 us; the launch traced here: 104 us
  blocking collectives  49.3 us (47%)
  starting transfers between devices  17.2 us (16%)
  Pallas kernels  16.5 us (16%)
  waiting for transfers between devices  12.6 us (12%)
  local copies, waits for them, and re-layouts  6.27 us (6%)
  other arithmetic  2.15 us (2%)
    all_to_all x1, blocking collectives, body(): piece = lax.all_to_all(source.transpose(1, 0, 2), 'plane', 0, 0, tiled=True)  17.4 us
    all_to_all x1, blocking collectives, body(): lax.all_to_all(radial_field, ('plane', 'ax'), 0, 0, tiled=True, axis_inde...  16.5 us
    all_to_all x1, blocking collectives, body(): lax.all_to_all(spatial.reshape(planes, local_t, radius_count), 'plane', 0...  15.4 us
    ppermute x3, starting transfers between devices, body(): other = lax.ppermute(jnp.stack([up, down]), 'ax', swap)  12.2 us
    all_to_all x1, waiting for transfers between devices, body(): lax.all_to_all(spectral, ('plane', 'ax'), 0, 0, tiled=True, axis_index_gr...  6.65 us
    ppermute x3, waiting for transfers between devices, body(): other = lax.ppermute(jnp.stack([up, down]), 'ax', swap)  5.99 us
    all_to_all x1, starting transfers between devices, body(): lax.all_to_all(spectral, ('plane', 'ax'), 0, 0, tiled=True, axis_index_gr...  5.01 us
    pallas_call x1, Pallas kernels, body(): pl.pallas_call(solve_kernel, out_shape=jax.ShapeDtypeStruct((span, size,...  4.86 us
  transfers between devices with their start and end apart: 4, of which 4 were waited for; matrix products, arithmetic and copies ran while one was open for 4% of the time, Pallas kernels for 0%

profile of v1, /device:TPU:8, one launch (start us, length us, event | category | flops | bytes accessed | tf_op | source)
XLA Modules:
  0.0 104.2 jit_solution(428667683547036182)
XLA Ops:
  0.0 1.2 %copy.16 = f32[64,16,128]{2,0,1:T(8,128)S(1)} copy(f32[64,16,128]{2,1,0:T(8,128)} %param.6) | data formatting | bytes 1048576 | tf_op args[0]
  1.2 0.0 copy-start.1
  1.2 17.4 %all_to_all.20 = f32[16,64,128]{2,1,0:T(8,128)} all-to-all(f32[16,64,128]{2,1,0:T(8,128)S(1)} %bitcast.55), channel_id=1, replica_groups=mesh['plane'=16,'ax'=16] {'plane'}, dimensions={0} | all-to-all | bytes 1048576 | tf_op jit(solution)/shard_map/all_to_all | solution.py:200
  18.6 4.0 %fourier_forward.1 = f32[32,32,128]{2,1,0:T(8,128)} custom-call(bf16[3,2,512,512]{3,2,1,0:T(8,128)(2,1)} %constant.58.clone.table_ref, f32[1024,128]{1,0:T(8,128)} %bitcast.57), custom_call_target="tpu_custom_call" | custom-call | tf_op jit(solution)/shard_map/fourier_forward/pallas_call | solution.py:201
  22.7 5.0 %all-to-all-start.1 = ((f32[32,32,128]{2,1,0:T(8,128)}), f32[32,32,128]{2,1,0:T(8,128)S(1)}, u32[]{:S(2)}, u32[]{:S(2)}) async-start(f32[32,32,128]{2,1,0:T(8,128)} %fourier_forward.1), calls=%async_computation.1 | async-start | bytes 1048576 | tf_op jit(solution)/shard_map/all_to_all | solution.py:208
  27.7 0.0 copy-done.1
  27.8 3.2 %constant_dynamic-slice_fusion.basis_ref = f32[32,128,128]{2,1,0:T(8,128)} fusion(f32[64,128,128]{2,1,0:T(8,128)} %param.7, s32[]{:T(128)S(6)} %select_n.246), kind=kLoop, calls=%fused_computation.57 | loop fusion | bytes 4194308 | tf_op jit(solution)/shard_map/dynamic_slice | solution.py:167
  30.9 0.6 fusion.9
  31.6 6.6 %all-to-all-done.1.x_ref = f32[32,32,128]{2,1,0:T(8,128)S(1)} async-done(((f32[32,32,128]{2,1,0:T(8,128)}), f32[32,32,128]{2,1,0:T(8,128)S(1)}, u32[]{:S(2)}, u32[]{:S(2)}) %all-to-all-start.1) | async-done | bytes 524320 | tf_op jit(solution)/shard_map/all_to_all | solution.py:208
  38.2 0.0 copy-start
  38.2 0.8 copy-done
  39.0 4.4 %radial_forward.1 = (f32[32,32,128]{2,1,0:T(8,128)}, f32[2,32,128]{2,1,0:T(8,128)}) custom-call(f32[32,32,128]{2,1,0:T(8,128)} %copy-done, f32[32,128,128]{2,1,0:T(8,128)} %constant_dynamic-slice_fusion.basis_ref, f32[1,128]{1,0:T(1,128)} %bitcast.60, f32[32,128]{1,0:T(8,128)} %get-tuple-element.16.decay_ref), custom_call_target="tpu_custom_call" | custom-call | tf_op jit(solution)/shard_map/radial_forward/pallas_call | solution.py:211
  43.4 1.9 %collective-permute-start = (f32[2,32,128]{2,1,0:T(8,128)}, f32[2,32,128]{2,1,0:T(8,128)S(1)}, u32[]{:S(2)}, u32[]{:S(2)}) collective-permute-start(f32[2,32,128]{2,1,0:T(8,128)} %get-tuple-element.8), channel_id=1, source_target_pairs={{0,2},{1,3},{2,0},{3,1},{4,6},{5,7},{6,4},{7,5},{8,10},{9,11},{10,... | collective-permute-start | bytes 98312 | tf_op jit(solution)/shard_map/ppermute | solution.py:230
  45.3 2.2 %collective-permute-done = f32[2,32,128]{2,1,0:T(8,128)S(1)} collective-permute-done((f32[2,32,128]{2,1,0:T(8,128)}, f32[2,32,128]{2,1,0:T(8,128)S(1)}, u32[]{:S(2)}, u32[]{:S(2)}) %collective-permute-start) | collective-permute-done | bytes 32800 | tf_op jit(solution)/shard_map/ppermute | solution.py:230
  47.5 0.8 add_select_fusion.5
  48.3 3.4 %collective-permute-start.1 = (f32[2,32,128]{2,1,0:T(8,128)S(1)}, f32[2,32,128]{2,1,0:T(8,128)S(1)}, u32[]{:S(2)}, u32[]{:S(2)}) collective-permute-start(f32[2,32,128]{2,1,0:T(8,128)S(1)} %pad_maximum_fusion), channel_id=1, source_target_pairs={{0,4},{1,5},{2,6},{3,7},{4,0},{5,1},{6,2},{7,3},{8,12},{9,13},{10,... | collective-permute-start | bytes 98312 | tf_op jit(solution)/shard_map/ppermute | solution.py:230
  51.6 1.9 %collective-permute-done.1 = f32[2,32,128]{2,1,0:T(8,128)S(1)} collective-permute-done((f32[2,32,128]{2,1,0:T(8,128)S(1)}, f32[2,32,128]{2,1,0:T(8,128)S(1)}, u32[]{:S(2)}, u32[]{:S(2)}) %collective-permute-start.1) | collective-permute-done | bytes 32800 | tf_op jit(solution)/shard_map/ppermute | solution.py:230
  53.6 6.9 %collective-permute-start.2 = (f32[2,32,128]{2,1,0:T(8,128)S(1)}, f32[2,32,128]{2,1,0:T(8,128)S(1)}, u32[]{:S(2)}, u32[]{:S(2)}) collective-permute-start(f32[2,32,128]{2,1,0:T(8,128)S(1)} %pad_maximum_fusion.1), channel_id=1, source_target_pairs={{0,8},{1,9},{2,10},{3,11},{4,12},{5,13},{6,14},{7,15},{8,0},{9,1},... | collective-permute-start | bytes 98312 | tf_op jit(solution)/shard_map/ppermute | solution.py:230
  60.5 1.9 %collective-permute-done.2 = f32[2,32,128]{2,1,0:T(8,128)S(1)} collective-permute-done((f32[2,32,128]{2,1,0:T(8,128)S(1)}, f32[2,32,128]{2,1,0:T(8,128)S(1)}, u32[]{:S(2)}, u32[]{:S(2)}) %collective-permute-start.2) | collective-permute-done | bytes 32800 | tf_op jit(solution)/shard_map/ppermute | solution.py:230
  62.5 0.1 fusion.4
  62.5 0.6 pad_maximum_fusion.2.start_ref
  63.2 4.9 %solve_and_radial_back.1 = f32[32,32,128]{2,1,0:T(8,128)} custom-call(f32[32,32,128]{2,1,0:T(8,128)} %get-tuple-element.7.f_ref, f32[32,128,128]{2,1,0:T(8,128)} %constant_dynamic-slice_fusion.basis_ref, f32[32,128]{1,0:T(8,128)} %get-tuple-element.16.decay_ref, f32[32,128]{1,0:T(8,128)} %get-tuple-element.15.gain_ref, f32[2,32,128]{2,1,0:T(8,128)} %pad_maximum_fusion.2.start_ref), custom_call_target="tpu_custom_call" | custom-call | tf_op jit(solution)/shard_map/solve_and_radial_back/pallas_call | solution.py:244
  68.0 16.5 %all_to_all.21.x_ref = f32[32,32,128]{2,1,0:T(8,128)} all-to-all(f32[32,32,128]{2,1,0:T(8,128)} %solve_and_radial_back.1), channel_id=1, replica_groups={{0,16,32,48,64,80,96,112,128,144,160,176,192,208,224,240,1,17,33,49,65,..., dimensions={0} | all-to-all | bytes 1048576 | tf_op jit(solution)/shard_map/all_to_all | solution.py:252
  84.5 3.2 %fourier_backward.1 = f32[1024,128]{1,0:T(8,128)} custom-call(bf16[2,2,512,512]{3,2,1,0:T(8,128)(2,1)} %constant.59.clone.table_ref, f32[32,32,128]{2,1,0:T(8,128)} %all_to_all.21.x_ref), custom_call_target="tpu_custom_call" | custom-call | tf_op jit(solution)/shard_map/fourier_backward/pallas_call | solution.py:255
  87.7 15.4 %all_to_all.22 = f32[16,64,128]{2,1,0:T(8,128)S(1)} all-to-all(f32[16,64,128]{2,1,0:T(8,128)} %bitcast.56), channel_id=1, replica_groups=mesh['plane'=16,'ax'=16] {'plane'}, dimensions={0} | all-to-all | bytes 1048576 | tf_op jit(solution)/shard_map/all_to_all | solution.py:262
  103.1 1.1 %copy.14 = f32[64,16,128]{2,1,0:T(8,128)} copy(f32[64,16,128]{2,0,1:T(8,128)S(1)} %bitcast.54) | data formatting | bytes 1048576 | tf_op jit(solution)/shard_map/transpose | solution.py:265
  (7 shorter events, 0.1 us)
Async XLA Ops:
  1.2 26.5 %copy-start.1 = (f32[64,128]{1,0:T(8,128)S(1)}, f32[64,128]{1,0:T(8,128)}, u32[]{:S(2)}) copy-start(f32[64,128]{1,0:T(8,128)} %param.9) | copy-start | bytes 98308
  22.7 15.5 %all-to-all-start.1 = ((f32[32,32,128]{2,1,0:T(8,128)}), f32[32,32,128]{2,1,0:T(8,128)S(1)}, u32[]{:S(2)}, u32[]{:S(2)}) async-start(f32[32,32,128]{2,1,0:T(8,128)} %fourier_forward.1), calls=%async_computation.1 | async-start | bytes 1048576 | tf_op jit(solution)/shard_map/all_to_all | solution.py:208
  38.2 0.8 copy-start
  43.4 4.1 %collective-permute-start = (f32[2,32,128]{2,1,0:T(8,128)}, f32[2,32,128]{2,1,0:T(8,128)S(1)}, u32[]{:S(2)}, u32[]{:S(2)}) collective-permute-start(f32[2,32,128]{2,1,0:T(8,128)} %get-tuple-element.8), channel_id=1, source_target_pairs={{0,2},{1,3},{2,0},{3,1},{4,6},{5,7},{6,4},{7,5},{8,10},{9,11},{10,... | collective-permute-start | bytes 98312 | tf_op jit(solution)/shard_map/ppermute | solution.py:230
  48.3 5.3 %collective-permute-start.1 = (f32[2,32,128]{2,1,0:T(8,128)S(1)}, f32[2,32,128]{2,1,0:T(8,128)S(1)}, u32[]{:S(2)}, u32[]{:S(2)}) collective-permute-start(f32[2,32,128]{2,1,0:T(8,128)S(1)} %pad_maximum_fusion), channel_id=1, source_target_pairs={{0,4},{1,5},{2,6},{3,7},{4,0},{5,1},{6,2},{7,3},{8,12},{9,13},{10,... | collective-permute-start | bytes 98312 | tf_op jit(solution)/shard_map/ppermute | solution.py:230
  53.6 8.8 %collective-permute-start.2 = (f32[2,32,128]{2,1,0:T(8,128)S(1)}, f32[2,32,128]{2,1,0:T(8,128)S(1)}, u32[]{:S(2)}, u32[]{:S(2)}) collective-permute-start(f32[2,32,128]{2,1,0:T(8,128)S(1)} %pad_maximum_fusion.1), channel_id=1, source_target_pairs={{0,8},{1,9},{2,10},{3,11},{4,12},{5,13},{6,14},{7,15},{8,0},{9,1},... | collective-permute-start | bytes 98312 | tf_op jit(solution)/shard_map/ppermute | solution.py:230

commit v2 on v1

v2 whole, which is shorter than its diff:
```python
import functools
import math

import jax
import jax.numpy as jnp
import ml_dtypes
import numpy as np
from jax import lax
from jax.experimental import pallas as pl
from jax.experimental.pallas import tpu as pltpu
from jax.sharding import PartitionSpec as P

axial_scale = 0.01
merge = 4
bf16 = jnp.bfloat16
f32 = jnp.float32
compact = pltpu.CompilerParams(vmem_limit_bytes=16 * 2**20)


def mode_order(total, planes, share):
    local = total // planes
    size = local // share
    share_at, plane_at, parity, half = np.meshgrid(
        np.arange(share), np.arange(planes), np.arange(2), np.arange(size // 2), indexing="ij"
    )
    return plane_at * local + share_at * size + 2 * half + parity


def fourier_halves(total, planes, share):
    order = mode_order(total, planes, share).transpose(2, 0, 1, 3).reshape(2, total // 2)
    angles = np.arange(total // 2)
    middle = total // 2
    harmonic = np.where(order <= middle, order, order - middle)
    radians = (harmonic[:, :, None] * angles % total) * (2.0 * math.pi / total)
    factor = np.where((order == 0) | (order == middle), math.sqrt(1.0 / total), math.sqrt(2.0 / total))
    waves = np.where((order <= middle)[:, :, None], np.cos(radians), np.sin(radians))
    return (waves * factor[:, :, None]).astype(np.float32)


def split_table(table):
    high = table.astype(ml_dtypes.bfloat16)
    rest = (table - high.astype(np.float32)).astype(ml_dtypes.bfloat16)
    return np.concatenate([high, rest], axis=2)


def split2(value):
    high = value.astype(bf16)
    return high, (value - high.astype(f32)).astype(bf16)


def split3(value):
    high = value.astype(bf16)
    rest = value - high.astype(f32)
    middle = rest.astype(bf16)
    return high, middle, (rest - middle.astype(f32)).astype(bf16)


def mul(left, right):
    return jnp.dot(left, right, preferred_element_type=f32)


def mul_t(left, right):
    return lax.dot_general(left, right, (((1,), (1,)), ((), ())), preferred_element_type=f32)


def twice(value, axis):
    return jnp.concatenate([value, value], axis=axis)


def swaps(teams):
    rounds = []
    reach = 1
    while reach < teams:
        if 2 * reach == teams and teams == 4:
            rounds.append([team ^ 3 for team in range(teams)])
        elif 2 * reach == teams and teams >= 8:
            wide = teams // 8
            far = (6, 7, 4, 5, 2, 3, 0, 1)
            rounds.append([far[team // wide] * wide + team % wide for team in range(teams)])
        else:
            rounds.append([team ^ reach for team in range(teams)])
        reach *= 2
    return rounds


def prepare_kernel(
    source_ref, shifts_ref, table_ref, out_ref, hold_ref, decay_ref, gain_ref, mix_ref, near_ref, end_ref,
    held_ref, shift_ref, sems, extra_sems,
):
    cells, angles, _ = out_ref.shape
    size = decay_ref.shape[0]
    rounds = near_ref.shape[0]
    teams = 2**rounds
    chunks = sems.shape[0]
    rows = angles // chunks
    shift_copy = pltpu.make_async_copy(shifts_ref, shift_ref, extra_sems.at[0])
    table_copy = pltpu.make_async_copy(table_ref, hold_ref, extra_sems.at[1])
    copies = [
        pltpu.make_async_copy(
            source_ref.at[pl.ds(chunk * rows, rows)], held_ref.at[pl.ds(chunk * rows, rows)], sems.at[chunk]
        )
        for chunk in range(chunks)
    ]
    shift_copy.start()
    for copy in copies:
        copy.start()
    table_copy.start()

    position = lax.axis_index("ax")
    block = lax.div(position, jnp.int32(merge))
    first = lax.rem(position, jnp.int32(merge)) * size
    shift_copy.wait()
    shifts = jnp.concatenate(
        [shift_ref[pl.ds(first + parity, size // 2, stride=2), :] for parity in range(2)], axis=0
    )
    rise = 0.5 * jnp.sqrt((2.0 + shifts) - 2.0)
    cosh_half = jnp.sqrt(1.0 + rise * rise)
    root = cosh_half - rise
    decay = root * root
    decay_ref[...] = decay
    gain_ref[...] = axial_scale / (4.0 * rise * cosh_half)
    one = jnp.ones_like(decay)
    zero = jnp.zeros_like(decay)
    powers = [power(decay, cells * merge)]
    for _ in range(rounds):
        powers.append(powers[-1] * powers[-1])
    whole_decay = powers[-1] * decay

    def step_power(count, bits):
        result = one
        for bit in range(bits):
            result = jnp.where((count & (1 << bit)) != 0, result * powers[bit], result)
        return result

    for turn in range(rounds):
        reach = 1 << turn
        above = (block & reach) != 0
        offset = block & (reach - 1)
        mine = jnp.where(above, one, powers[turn])
        theirs = jnp.where(above, powers[turn], one)
        mix_ref[turn, 0, 0] = mine
        mix_ref[turn, 0, 1] = theirs
        mix_ref[turn, 1, 0] = theirs
        mix_ref[turn, 1, 1] = mine
        near_ref[turn, 0] = jnp.where(above, step_power(offset, turn), zero)
        near_ref[turn, 1] = jnp.where(above, zero, step_power(reach - 1 - offset, turn))
    closing = decay / (1.0 - whole_decay * whole_decay)
    to_first = closing * step_power(block, rounds)
    to_last = closing * step_power(teams - 1 - block, rounds)
    end_ref[0, 0] = to_first * whole_decay
    end_ref[0, 1] = -to_first
    end_ref[1, 0] = -to_last
    end_ref[1, 1] = to_last * whole_decay

    for chunk, copy in enumerate(copies):
        copy.wait()
        part = pl.ds(chunk * rows, rows)
        for cell in range(cells):
            out_ref[cell, part, :] = held_ref[part, cell, :]
    table_copy.wait()


def power(base, count):
    result = None
    while count:
        if count & 1:
            result = base if result is None else result * base
        base = base * base
        count >>= 1
    return result


def forward_kernel(table_ref, x_ref, out_ref):
    half_t = x_ref.shape[0] // 2
    width = x_ref.shape[1]
    blocks, size, _ = out_ref.shape
    low, high = x_ref[:half_t], x_ref[half_t:]
    for parity in range(2):
        folded = low + high if parity == 0 else low - high
        a, b, c = split3(folded)
        first = mul(table_ref[parity], twice(jnp.concatenate([a, b], axis=1), 0))
        result = first[:, :width] + (first[:, width:] + mul(table_ref[parity, :, :half_t], c))
        out_ref[:, parity * (size // 2) : (parity + 1) * (size // 2), :] = result.reshape(
            blocks, size // 2, width
        )


def backward_kernel(table_ref, x_ref, out_ref):
    blocks, size, width = x_ref.shape
    half_k = blocks * size // 2
    sums = []
    for parity in range(2):
        part = x_ref[:, parity * (size // 2) : (parity + 1) * (size // 2), :].reshape(-1, width)
        a, b = split2(part)
        first = mul(table_ref[parity, :, :half_k], jnp.concatenate([a, b], axis=1))
        sums.append(first[:, :width] + (first[:, width:] + mul(table_ref[parity, :, half_k:], a)))
    half_t = out_ref.shape[0] // 2
    out_ref[:half_t] = sums[0] + sums[1]
    out_ref[half_t:] = sums[0] - sums[1]


def first_mode(size):
    return lax.rem(lax.axis_index("ax"), jnp.int32(merge)) * size


def modal_kernel(x_ref, basis_ref, weights_ref, decay_ref, f_ref, carry_ref):
    depth, size, _ = x_ref.shape
    weights = weights_ref[...]
    first = first_mode(size)
    for place in range(size):
        parity, half = divmod(place, size // 2)
        values = jnp.concatenate(split3(x_ref[:, place, :] * weights), axis=0)
        basis = jnp.concatenate(split2(basis_ref[first + (2 * half + parity)]), axis=0)
        result = mul(twice(values, 1), basis)
        f_ref[:, place, :] = result[:depth] + (result[depth : 2 * depth] + result[2 * depth :])
    decay = decay_ref[...]
    up = f_ref[0]
    down = f_ref[depth - 1]
    for step in range(1, depth):
        up = up * decay + f_ref[step]
        down = down * decay + f_ref[depth - 1 - step]
    carry_ref[0] = up
    carry_ref[1] = down


def solve_kernel(f_ref, basis_ref, decay_ref, gain_ref, mix_ref, near_ref, end_ref, carry_ref, *refs):
    *other_refs, out_ref, up_ref, down_ref = refs
    depth, size, _ = f_ref.shape
    decay = decay_ref[...]
    first = first_mode(size)
    total = [carry_ref[0], carry_ref[1]]
    start = [jnp.zeros_like(decay)] * 2
    for turn, other_ref in enumerate(other_refs):
        other = [other_ref[0], other_ref[1]]
        start = [start[end] + near_ref[turn, end] * other[end] for end in range(2)]
        total = [mix_ref[turn, 0, end] * total[end] + mix_ref[turn, 1, end] * other[end] for end in range(2)]
    up, down = (start[end] + (end_ref[end, 0] * total[0] + end_ref[end, 1] * total[1]) for end in range(2))
    for step in range(depth):
        up = up * decay
        up_ref[step] = up
        up = up + f_ref[step]
        down = down * decay + f_ref[depth - 1 - step]
        down_ref[depth - 1 - step] = down
    for place in range(size):
        parity, half = divmod(place, size // 2)
        field = (up_ref[:, place, :] + down_ref[:, place, :]) * gain_ref[place : place + 1, :]
        values = jnp.concatenate(split2(field), axis=0)
        basis = jnp.concatenate(split2(basis_ref[first + (2 * half + parity)]), axis=1)
        result = mul_t(twice(values, 1), basis)
        out_ref[:, place, :] = result[:depth] + result[depth:]


def scatter_kernel(x_ref, out_ref, row_sems):
    rows = [
        pltpu.make_async_copy(x_ref.at[cell], out_ref.at[:, cell], row_sems.at[cell])
        for cell in range(x_ref.shape[0])
    ]
    for copy in rows:
        copy.start()
    for copy in rows:
        copy.wait()


def whole(memory_space=pltpu.VMEM):
    return pl.BlockSpec(memory_space=memory_space)


def in_vmem(value):
    return pltpu.with_memory_space_constraint(value, pltpu.VMEM)


def in_hbm(value):
    return pltpu.with_memory_space_constraint(value, pltpu.HBM)


def body(source, radial_basis, radial_weights, mode_shifts):
    planes = lax.axis_size("plane")
    blocks = lax.axis_size("ax")
    local_t, depth_cells, radius_count = source.shape
    total_t = local_t * planes
    size = local_t // merge
    span = depth_cells * merge
    teams = blocks // merge
    table = fourier_halves(total_t, planes, merge)
    forward_table = jnp.asarray(split_table(table))
    backward_table = jnp.asarray(split_table(table.transpose(0, 2, 1)))
    neighbours = [
        [plane * blocks + first + share for share in range(merge) for plane in range(planes)]
        for first in range(0, blocks, merge)
    ]
    rounds = swaps(teams)

    turned, held_table, decay, gain, mix, near, ends = pl.pallas_call(
        prepare_kernel,
        out_shape=(
            pltpu.VMEM((depth_cells, local_t, radius_count), f32),
            pltpu.VMEM(forward_table.shape, bf16),
            pltpu.VMEM((size, radius_count), f32),
            pltpu.VMEM((size, radius_count), f32),
            pltpu.VMEM((len(rounds), 2, 2, size, radius_count), f32),
            pltpu.VMEM((len(rounds), 2, size, radius_count), f32),
            pltpu.VMEM((2, 2, size, radius_count), f32),
        ),
        in_specs=[whole(pltpu.HBM)] * 3,
        out_specs=(whole(),) * 7,
        scratch_shapes=[
            pltpu.VMEM(source.shape, f32),
            pltpu.VMEM(mode_shifts.shape, f32),
            pltpu.SemaphoreType.DMA((4,)),
            pltpu.SemaphoreType.DMA((2,)),
        ],
        name="cells_first",
        compiler_params=compact,
    )(in_hbm(source), in_hbm(mode_shifts), in_hbm(forward_table))
    piece = lax.all_to_all(turned, "plane", 0, 0, tiled=True)
    spectral = pl.pallas_call(
        forward_kernel,
        out_shape=pltpu.VMEM((planes * merge, size, radius_count), f32),
        in_specs=[whole()] * 2,
        out_specs=whole(),
        name="fourier_forward",
        compiler_params=compact,
    )(in_vmem(held_table), in_vmem(piece.reshape(total_t, radius_count)))
    modal = lax.all_to_all(
        spectral, ("plane", "ax"), 0, 0, tiled=True, axis_index_groups=neighbours
    )
    spectra, carries = pl.pallas_call(
        modal_kernel,
        out_shape=(
            pltpu.VMEM((span, size, radius_count), f32),
            pltpu.VMEM((2, size, radius_count), f32),
        ),
        in_specs=[whole()] * 4,
        out_specs=(whole(), whole()),
        name="radial_forward",
        compiler_params=compact,
    )(in_vmem(modal), in_vmem(radial_basis), radial_weights.reshape(1, radius_count), in_vmem(decay))
    others = []
    sent = carries
    for turn, partners in enumerate(rounds):
        if turn:
            sent = mix[turn - 1, 0] * sent + mix[turn - 1, 1] * others[-1]
        pairs = [
            (team * merge + share, partner * merge + share)
            for team, partner in enumerate(partners)
            for share in range(merge)
        ]
        others.append(lax.ppermute(sent, "ax", pairs))
    radial_field = pl.pallas_call(
        solve_kernel,
        out_shape=pltpu.VMEM((span, size, radius_count), f32),
        in_specs=[whole()] * (8 + len(rounds)),
        out_specs=whole(),
        scratch_shapes=[pltpu.VMEM((span, size, radius_count), f32)] * 2,
        name="solve_and_radial_back",
        compiler_params=compact,
    )(
        in_vmem(spectra),
        in_vmem(radial_basis),
        in_vmem(decay),
        in_vmem(gain),
        in_vmem(mix),
        in_vmem(near),
        in_vmem(ends),
        in_vmem(carries),
        *map(in_vmem, others),
    )
    collected = lax.all_to_all(
        radial_field, ("plane", "ax"), 0, 0, tiled=True, axis_index_groups=neighbours
    )
    spatial = pl.pallas_call(
        backward_kernel,
        out_shape=pltpu.VMEM((total_t, radius_count), f32),
        in_specs=[whole()] * 2,
        out_specs=whole(),
        name="fourier_backward",
        compiler_params=compact,
    )(in_vmem(backward_table), in_vmem(collected))
    pressure = lax.all_to_all(
        spatial.reshape(planes, local_t, radius_count), "plane", 0, 0, tiled=True
    )
    return pl.pallas_call(
        scatter_kernel,
        out_shape=jax.ShapeDtypeStruct(source.shape, f32),
        in_specs=[whole()],
        out_specs=whole(pltpu.HBM),
        scratch_shapes=[pltpu.SemaphoreType.DMA((depth_cells,))],
        name="angles_first",
        compiler_params=compact,
    )(in_vmem(pressure))


def solution(mesh):
    placed = (P("plane", "ax", None), P("plane", None, None), P(), P("plane", None))
    return jax.shard_map(
        body, mesh=mesh, in_specs=placed, out_specs=P("plane", "ax", None), check_vma=False
    )
```

time: 105 us -> 86.1 us (0.82)
  blocking collectives: 49.3 us -> 66.5 us
  Pallas kernels: 16.5 us -> 7.02 us
  waiting for transfers between devices: 12.6 us -> 3.45 us
  starting transfers between devices: 17.2 us -> 8.48 us
  local copies, waits for them, and re-layouts: 6.27 us -> 0.01 us
  other arithmetic: 2.15 us -> 0.01 us
    all_to_all x1 -> x2, blocking collectives: 17.4 us -> 35.5 us  [the longest x1 18.2 us: body(): lax.all_to_all(spectral, ('plane', 'ax'), 0, 0, tiled=True, axis_index_gr...]
    pallas_call x4 -> x6, Pallas kernels: 16.5 us -> 7.02 us  [the longest x1 1.94 us: body(): pl.pallas_call(prepare_kernel, out_shape=(pltpu.VMEM((depth_cells, local_...]
    all_to_all x1 -> x0, waiting for transfers between devices: 6.65 us -> none  [body(): lax.all_to_all(spectral, ('plane', 'ax'), 0, 0, tiled=True, axis_index_gr...]
    all_to_all x1 -> x0, starting transfers between devices: 5.01 us -> none  [body(): lax.all_to_all(spectral, ('plane', 'ax'), 0, 0, tiled=True, axis_index_gr...]
    ppermute x3 -> x2, starting transfers between devices: 12.2 us -> 8.48 us  [body(): others.append(lax.ppermute(sent, 'ax', pairs))]
    dynamic_slice x1 -> x0, local copies, waits for them, and re-layouts: 3.15 us -> none  [body(): basis = lax.dynamic_slice_in_dim(radial_basis, share * size, size, 0)]
    ppermute x3 -> x2, waiting for transfers between devices: 5.99 us -> 3.45 us  [body(): others.append(lax.ppermute(sent, 'ax', pairs))]
    unnamed x5 -> x6, local copies, waits for them, and re-layouts: 2.01 us -> 0.01 us
  transfers between devices with their start and end apart: 4 -> 2, of which waited for: 4 -> 2; matrix products, arithmetic and copies ran while one was open for 4% -> 0% of each run, Pallas kernels for 0% -> 0%
where the time goes in v2:
time: 86.1 us; the launch traced here: 85.5 us
  blocking collectives  66.5 us (77%)
  starting transfers between devices  8.48 us (10%)
  Pallas kernels  7.02 us (8%)
  waiting for transfers between devices  3.45 us (4%)
    all_to_all x1, blocking collectives, body(): lax.all_to_all(spectral, ('plane', 'ax'), 0, 0, tiled=True, axis_index_gr...  18.2 us
    all_to_all x1, blocking collectives, body(): piece = lax.all_to_all(turned, 'plane', 0, 0, tiled=True)  17.3 us
    all_to_all x1, blocking collectives, body(): lax.all_to_all(radial_field, ('plane', 'ax'), 0, 0, tiled=True, axis_inde...  16.5 us
    all_to_all x1, blocking collectives, body(): lax.all_to_all(spatial.reshape(planes, local_t, radius_count), 'plane', 0...  14.6 us
    ppermute x2, starting transfers between devices, body(): others.append(lax.ppermute(sent, 'ax', pairs))  8.48 us
    ppermute x2, waiting for transfers between devices, body(): others.append(lax.ppermute(sent, 'ax', pairs))  3.45 us
    pallas_call x1, Pallas kernels, body(): pl.pallas_call(prepare_kernel, out_shape=(pltpu.VMEM((depth_cells, local_...  1.94 us
  transfers between devices with their start and end apart: 2, of which 2 were waited for; matrix products, arithmetic and copies ran while one was open for 0% of the time, Pallas kernels for 0%

profile of v2, /device:TPU:8, one launch (start us, length us, event | category | flops | bytes accessed | tf_op | source)
XLA Modules:
  0.0 85.5 jit_solution(16962529909912998235)
XLA Ops:
  0.0 1.9 %cells_first.1 = (f32[16,64,128]{2,1,0:T(8,128)S(1)}, bf16[2,512,1024]{2,1,0:T(8,128)(2,1)S(1)}, f32[16,128]{1,0:T(8,128)S(1)}, f32[16,128]{1,0:T(8,128)S(1)}, f...) custom-call(f32[64,16,128]{2,1,0:T(8,128)} %source_ref.1, ...), custom_call_target="tpu_custom_call" | custom-call | tf_op jit(solution)/shard_map/cells_first/pallas_call | solution.py:293
  2.0 17.3 %all_to_all.20 = f32[16,64,128]{2,1,0:T(8,128)S(1)} all-to-all(f32[16,64,128]{2,1,0:T(8,128)S(1)} %get-tuple-element.15), channel_id=1, replica_groups=mesh['plane'=16,'ax'=16] {'plane'}, dimensions={0} | all-to-all | bytes 1048576 | tf_op jit(solution)/shard_map/all_to_all | solution.py:315
  19.3 0.0 copy-start
  19.3 0.0 copy-start.2
  19.3 1.0 %fourier_forward.1 = f32[64,16,128]{2,1,0:T(8,128)S(1)} custom-call(bf16[2,512,1024]{2,1,0:T(8,128)(2,1)S(1)} %get-tuple-element.14.table_ref, f32[1024,128]{1,0:T(8,128)S(1)} %bitcast.11), custom_call_target="tpu_custom_call" | custom-call | tf_op jit(solution)/shard_map/fourier_forward/pallas_call | solution.py:316
  20.3 18.2 %all_to_all.21.x_ref = f32[64,16,128]{2,1,0:T(8,128)S(1)} all-to-all(f32[64,16,128]{2,1,0:T(8,128)S(1)} %fourier_forward.1), channel_id=1, replica_groups={{0,16,32,48,64,80,96,112,128,144,160,176,192,208,224,240,1,17,33,49,65,..., dimensions={0} | all-to-all | bytes 1048576 | tf_op jit(solution)/shard_map/all_to_all | solution.py:324
  38.4 0.0 copy-done
  38.4 0.0 copy-done.2
  38.4 1.2 %radial_forward.1 = (f32[64,16,128]{2,1,0:T(8,128)S(1)}, f32[2,16,128]{2,1,0:T(8,128)S(1)}) custom-call(f32[64,16,128]{2,1,0:T(8,128)S(1)} %all_to_all.21.x_ref, f32[64,128,128]{2,1,0:T(8,128)S(1)} %copy-done, f32[1,128]{1,0:T(1,128)S(1)} %bitcast.13, f32[16,128]{1,0:T(8,128)S(1)} %get-tuple-element.16.decay_ref), custom_call_target="tpu_custom_call" | custom-call | tf_op jit(solution)/shard_map/radial_forward/pallas_call | solution.py:327
  39.6 3.4 %collective-permute-start = (f32[2,16,128]{2,1,0:T(8,128)S(1)}, f32[2,16,128]{2,1,0:T(8,128)S(1)}, u32[]{:S(2)}, u32[]{:S(2)}) collective-permute-start(f32[2,16,128]{2,1,0:T(8,128)S(1)} %get-tuple-element.22.carry_ref), channel_id=1, source_target_pairs={{0,4},{1,5},{2,6},{3,7},{4,0},{5,1},{6,2},{7,3},{8,12},{9,13},{10,... | collective-permute-start | bytes 49160 | tf_op jit(solution)/shard_map/ppermute | solution.py:348
  43.0 1.7 %collective-permute-done.refs_0_ = f32[2,16,128]{2,1,0:T(8,128)S(1)} collective-permute-done((f32[2,16,128]{2,1,0:T(8,128)S(1)}, f32[2,16,128]{2,1,0:T(8,128)S(1)}, u32[]{:S(2)}, u32[]{:S(2)}) %collective-permute-start) | collective-permute-done | bytes 16416 | tf_op jit(solution)/shard_map/ppermute | solution.py:348
  44.7 5.1 %collective-permute-start.1 = (f32[2,16,128]{2,1,0:T(8,128)S(1)}, f32[2,16,128]{2,1,0:T(8,128)S(1)}, u32[]{:S(2)}, u32[]{:S(2)}) collective-permute-start(f32[2,16,128]{2,1,0:T(8,128)S(1)} %fusion), channel_id=1, source_target_pairs={{0,12},{1,13},{2,14},{3,15},{4,8},{5,9},{6,10},{7,11},{8,4},{9,5},... | collective-permute-start | bytes 49160 | tf_op jit(solution)/shard_map/ppermute | solution.py:348
  49.8 1.7 %collective-permute-done.1.refs_1_ = f32[2,16,128]{2,1,0:T(8,128)S(1)} collective-permute-done((f32[2,16,128]{2,1,0:T(8,128)S(1)}, f32[2,16,128]{2,1,0:T(8,128)S(1)}, u32[]{:S(2)}, u32[]{:S(2)}) %collective-permute-start.1) | collective-permute-done | bytes 16416 | tf_op jit(solution)/shard_map/ppermute | solution.py:348
  51.5 0.0 copy-start.1
  51.6 1.3 %solve_and_radial_back.1 = f32[64,16,128]{2,1,0:T(8,128)S(1)} custom-call(f32[64,16,128]{2,1,0:T(8,128)S(1)} %get-tuple-element.17.f_ref, f32[64,128,128]{2,1,0:T(8,128)S(1)} %copy-done, f32[16,128]{1,0:T(8,128)S(1)} %get-tuple-element.16.decay_ref, f32[16,128]{1,0:T(8,128)S(1)} %get-tuple-element.18.gain_ref, ...), custom_call_target="tpu_custom_call" | custom-call | tf_op jit(solution)/shard_map/solve_and_radial_back/pallas_call | solution.py:349
  52.8 16.5 %all_to_all.22.x_ref = f32[64,16,128]{2,1,0:T(8,128)S(1)} all-to-all(f32[64,16,128]{2,1,0:T(8,128)S(1)} %solve_and_radial_back.1), channel_id=1, replica_groups={{0,16,32,48,64,80,96,112,128,144,160,176,192,208,224,240,1,17,33,49,65,..., dimensions={0} | all-to-all | bytes 1048576 | tf_op jit(solution)/shard_map/all_to_all | solution.py:368
  69.3 0.0 copy-done.1
  69.3 0.7 fourier_backward.1
  70.0 14.6 %all_to_all.23.x_ref = f32[16,64,128]{2,1,0:T(8,128)S(1)} all-to-all(f32[16,64,128]{2,1,0:T(8,128)S(1)} %bitcast.12), channel_id=1, replica_groups=mesh['plane'=16,'ax'=16] {'plane'}, dimensions={0} | all-to-all | bytes 1048576 | tf_op jit(solution)/shard_map/all_to_all | solution.py:379
  84.6 0.9 %angles_first.1 = f32[64,16,128]{2,1,0:T(8,128)} custom-call(f32[16,64,128]{2,1,0:T(8,128)S(1)} %all_to_all.23.x_ref), custom_call_target="tpu_custom_call" | custom-call | tf_op jit(solution)/shard_map/angles_first/pallas_call | solution.py:382
  (1 shorter events, 0.0 us)
Async XLA Ops:
  19.3 19.2 %copy-start = (f32[64,128,128]{2,1,0:T(8,128)S(1)}, f32[64,128,128]{2,1,0:T(8,128)}, u32[]{:S(2)}) copy-start(f32[64,128,128]{2,1,0:T(8,128)} %basis_ref.3) | copy-start | bytes 12582916
  19.3 19.2 %copy-start.2 = (f32[128]{0:T(128)S(1)}, f32[128]{0:T(128)}, u32[]{:S(2)}) copy-start(f32[128]{0:T(128)} %param.8) | copy-start | bytes 1540
  39.6 5.1 %collective-permute-start = (f32[2,16,128]{2,1,0:T(8,128)S(1)}, f32[2,16,128]{2,1,0:T(8,128)S(1)}, u32[]{:S(2)}, u32[]{:S(2)}) collective-permute-start(f32[2,16,128]{2,1,0:T(8,128)S(1)} %get-tuple-element.22.carry_ref), channel_id=1, source_target_pairs={{0,4},{1,5},{2,6},{3,7},{4,0},{5,1},{6,2},{7,3},{8,12},{9,13},{10,... | collective-permute-start | bytes 49160 | tf_op jit(solution)/shard_map/ppermute | solution.py:348
  44.7 6.8 %collective-permute-start.1 = (f32[2,16,128]{2,1,0:T(8,128)S(1)}, f32[2,16,128]{2,1,0:T(8,128)S(1)}, u32[]{:S(2)}, u32[]{:S(2)}) collective-permute-start(f32[2,16,128]{2,1,0:T(8,128)S(1)} %fusion), channel_id=1, source_target_pairs={{0,12},{1,13},{2,14},{3,15},{4,8},{5,9},{6,10},{7,11},{8,4},{9,5},... | collective-permute-start | bytes 49160 | tf_op jit(solution)/shard_map/ppermute | solution.py:348
  51.5 17.7 %copy-start.1 = (bf16[2,512,1024]{2,1,0:T(8,128)(2,1)S(1)}, bf16[2,512,1024]{2,1,0:T(8,128)(2,1)}, u32[]{:S(2)}) copy-start(bf16[2,512,1024]{2,1,0:T(8,128)(2,1)} %constant.5.clone.table_ref) | copy-start | bytes 6291460

commit v3 on v2

--- a/solution.py
+++ b/solution.py
@@ -11,7 +11,8 @@
 from jax.sharding import PartitionSpec as P
 
 axial_scale = 0.01
-merge = 4
+cores = 2
+merge = 2
 bf16 = jnp.bfloat16
 f32 = jnp.float32
 compact = pltpu.CompilerParams(vmem_limit_bytes=16 * 2**20)
@@ -84,7 +85,7 @@
 
 
 def prepare_kernel(
-    source_ref, shifts_ref, table_ref, out_ref, hold_ref, decay_ref, gain_ref, mix_ref, near_ref, end_ref,
+    source_ref, shifts_ref, table_ref, out_ref, hold_ref, decay_ref, gain_ref, link_ref, lead_ref, mix_ref, near_ref, end_ref,
     held_ref, shift_ref, sems, extra_sems,
 ):
     cells, angles, _ = out_ref.shape
@@ -106,9 +107,8 @@
         copy.start()
     table_copy.start()
 
-    position = lax.axis_index("ax")
-    block = lax.div(position, jnp.int32(merge))
-    first = lax.rem(position, jnp.int32(merge)) * size
+    core, share, team = place_in_team()
+    first = share * size
     shift_copy.wait()
     shifts = jnp.concatenate(
         [shift_ref[pl.ds(first + parity, size // 2, stride=2), :] for parity in range(2)], axis=0
@@ -121,7 +121,34 @@
     gain_ref[...] = axial_scale / (4.0 * rise * cosh_half)
     one = jnp.ones_like(decay)
     zero = jnp.zeros_like(decay)
-    powers = [power(decay, cells * merge)]
+
+    inner = [one, power(decay, cells)]
+    for _ in range(2):
+        inner.append(inner[-1] * inner[1])
+    on_first = core == 0
+
+    def apart(distance):
+        below = inner[-distance - 1] if distance < 0 else zero
+        above = inner[distance - 1] if distance > 0 else zero
+        return below, above
+
+    for source in range(merge):
+        for target in range(merge):
+            gap = 2 * (source - target)
+            for end in range(2):
+                link_ref[0, target, source, end] = apart(gap)[end]
+                link_ref[1, target, source, end] = jnp.where(
+                    on_first, apart(gap + 1)[end], apart(gap - 1)[end]
+                )
+        early, late = 2 * source, 2 * source + 1
+        for owner in range(2):
+            near, far = (early, late) if owner == 0 else (late, early)
+            link_ref[owner, merge, source, 0] = jnp.where(on_first, inner[3 - near], inner[3 - far])
+            link_ref[owner, merge, source, 1] = jnp.where(on_first, inner[near], inner[far])
+        lead_ref[source, 0] = jnp.where(on_first, inner[early], inner[late])
+        lead_ref[source, 1] = jnp.where(on_first, inner[3 - early], inner[3 - late])
+
+    powers = [inner[3] * inner[1]]
     for _ in range(rounds):
         powers.append(powers[-1] * powers[-1])
     whole_decay = powers[-1] * decay
@@ -134,8 +161,8 @@
 
     for turn in range(rounds):
         reach = 1 << turn
-        above = (block & reach) != 0
-        offset = block & (reach - 1)
+        above = (team & reach) != 0
+        offset = team & (reach - 1)
         mine = jnp.where(above, one, powers[turn])
         theirs = jnp.where(above, powers[turn], one)
         mix_ref[turn, 0, 0] = mine
@@ -145,8 +172,8 @@
         near_ref[turn, 0] = jnp.where(above, step_power(offset, turn), zero)
         near_ref[turn, 1] = jnp.where(above, zero, step_power(reach - 1 - offset, turn))
     closing = decay / (1.0 - whole_decay * whole_decay)
-    to_first = closing * step_power(block, rounds)
-    to_last = closing * step_power(teams - 1 - block, rounds)
+    to_first = closing * step_power(team, rounds)
+    to_last = closing * step_power(teams - 1 - team, rounds)
     end_ref[0, 0] = to_first * whole_decay
     end_ref[0, 1] = -to_first
     end_ref[1, 0] = -to_last
@@ -158,6 +185,13 @@
         for cell in range(cells):
             out_ref[cell, part, :] = held_ref[part, cell, :]
     table_copy.wait()
+
+
+def place_in_team():
+    position = lax.axis_index("ax")
+    core = lax.rem(position, jnp.int32(cores))
+    chip = lax.div(position, jnp.int32(cores))
+    return core, lax.rem(chip, jnp.int32(merge)), lax.div(chip, jnp.int32(merge))
 
 
 def power(base, count):
@@ -199,14 +233,10 @@
     out_ref[half_t:] = sums[0] - sums[1]
 
 
-def first_mode(size):
-    return lax.rem(lax.axis_index("ax"), jnp.int32(merge)) * size
-
-
 def modal_kernel(x_ref, basis_ref, weights_ref, decay_ref, f_ref, carry_ref):
     depth, size, _ = x_ref.shape
     weights = weights_ref[...]
-    first = first_mode(size)
+    first = place_in_team()[1] * size
     for place in range(size):
         parity, half = divmod(place, size // 2)
         values = jnp.concatenate(split3(x_ref[:, place, :] * weights), axis=0)
@@ -214,33 +244,54 @@
         result = mul(twice(values, 1), basis)
         f_ref[:, place, :] = result[:depth] + (result[depth : 2 * depth] + result[2 * depth :])
     decay = decay_ref[...]
-    up = f_ref[0]
-    down = f_ref[depth - 1]
-    for step in range(1, depth):
-        up = up * decay + f_ref[step]
-        down = down * decay + f_ref[depth - 1 - step]
-    carry_ref[0] = up
-    carry_ref[1] = down
-
-
-def solve_kernel(f_ref, basis_ref, decay_ref, gain_ref, mix_ref, near_ref, end_ref, carry_ref, *refs):
+    part = depth // merge
+    ups = [f_ref[which * part] for which in range(merge)]
+    downs = [f_ref[which * part + part - 1] for which in range(merge)]
+    for step in range(1, part):
+        for which in range(merge):
+            ups[which] = ups[which] * decay + f_ref[which * part + step]
+            downs[which] = downs[which] * decay + f_ref[which * part + part - 1 - step]
+    for which in range(merge):
+        carry_ref[which, 0] = ups[which]
+        carry_ref[which, 1] = downs[which]
+
+
+def solve_kernel(
+    f_ref, basis_ref, decay_ref, gain_ref, link_ref, lead_ref, mix_ref, near_ref, end_ref, carry_ref, twin_ref, *refs
+):
     *other_refs, out_ref, up_ref, down_ref = refs
     depth, size, _ = f_ref.shape
+    part = depth // merge
     decay = decay_ref[...]
-    first = first_mode(size)
-    total = [carry_ref[0], carry_ref[1]]
+    first = place_in_team()[1] * size
+
+    def within_team(target, end):
+        terms = [
+            link_ref[owner, target, source, end] * ref[source, end]
+            for owner, ref in enumerate((carry_ref, twin_ref))
+            for source in range(merge)
+        ]
+        return functools.reduce(jnp.add, terms)
+
+    total = [within_team(merge, end) for end in range(2)]
     start = [jnp.zeros_like(decay)] * 2
     for turn, other_ref in enumerate(other_refs):
         other = [other_ref[0], other_ref[1]]
         start = [start[end] + near_ref[turn, end] * other[end] for end in range(2)]
         total = [mix_ref[turn, 0, end] * total[end] + mix_ref[turn, 1, end] * other[end] for end in range(2)]
-    up, down = (start[end] + (end_ref[end, 0] * total[0] + end_ref[end, 1] * total[1]) for end in range(2))
-    for step in range(depth):
-        up = up * decay
-        up_ref[step] = up
-        up = up + f_ref[step]
-        down = down * decay + f_ref[depth - 1 - step]
-        down_ref[depth - 1 - step] = down
+    start = [start[end] + (end_ref[end, 0] * total[0] + end_ref[end, 1] * total[1]) for end in range(2)]
+    ups, downs = (
+        [within_team(which, end) + lead_ref[which, end] * start[end] for which in range(merge)] for end in range(2)
+    )
+    for step in range(part):
+        for which in range(merge):
+            low = which * part + step
+            high = which * part + part - 1 - step
+            ups[which] = ups[which] * decay
+            up_ref[low] = ups[which]
+            ups[which] = ups[which] + f_ref[low]
+            downs[which] = downs[which] * decay + f_ref[high]
+            down_ref[high] = downs[which]
     for place in range(size):
         parity, half = divmod(place, size // 2)
         field = (up_ref[:, place, :] + down_ref[:, place, :]) * gain_ref[place : place + 1, :]
@@ -280,29 +331,36 @@
     total_t = local_t * planes
     size = local_t // merge
     span = depth_cells * merge
-    teams = blocks // merge
+    teams = blocks // (merge * cores)
     table = fourier_halves(total_t, planes, merge)
     forward_table = jnp.asarray(split_table(table))
     backward_table = jnp.asarray(split_table(table.transpose(0, 2, 1)))
     neighbours = [
-        [plane * blocks + first + share for share in range(merge) for plane in range(planes)]
-        for first in range(0, blocks, merge)
+        [
+            plane * blocks + (team * merge + share) * cores + core
+            for share in range(merge)
+            for plane in range(planes)
+        ]
+        for team in range(teams)
+        for core in range(cores)
     ]
     rounds = swaps(teams)
 
-    turned, held_table, decay, gain, mix, near, ends = pl.pallas_call(
+    turned, held_table, decay, gain, link, lead, mix, near, ends = pl.pallas_call(
         prepare_kernel,
         out_shape=(
             pltpu.VMEM((depth_cells, local_t, radius_count), f32),
             pltpu.VMEM(forward_table.shape, bf16),
             pltpu.VMEM((size, radius_count), f32),
             pltpu.VMEM((size, radius_count), f32),
+            pltpu.VMEM((2, merge + 1, merge, 2, size, radius_count), f32),
+            pltpu.VMEM((merge, 2, size, radius_count), f32),
             pltpu.VMEM((len(rounds), 2, 2, size, radius_count), f32),
             pltpu.VMEM((len(rounds), 2, size, radius_count), f32),
             pltpu.VMEM((2, 2, size, radius_count), f32),
         ),
         in_specs=[whole(pltpu.HBM)] * 3,
-        out_specs=(whole(),) * 7,
+        out_specs=(whole(),) * 9,
         scratch_shapes=[
             pltpu.VMEM(source.shape, f32),
             pltpu.VMEM(mode_shifts.shape, f32),
@@ -328,28 +386,30 @@
         modal_kernel,
         out_shape=(
             pltpu.VMEM((span, size, radius_count), f32),
-            pltpu.VMEM((2, size, radius_count), f32),
+            pltpu.VMEM((merge, 2, size, radius_count), f32),
         ),
         in_specs=[whole()] * 4,
         out_specs=(whole(), whole()),
         name="radial_forward",
         compiler_params=compact,
     )(in_vmem(modal), in_vmem(radial_basis), radial_weights.reshape(1, radius_count), in_vmem(decay))
+    twin = lax.ppermute(carries, "ax", [(index, index ^ 1) for index in range(blocks)])
+    sent = (link[0, merge] * carries + link[1, merge] * twin).sum(axis=0)
     others = []
-    sent = carries
     for turn, partners in enumerate(rounds):
         if turn:
             sent = mix[turn - 1, 0] * sent + mix[turn - 1, 1] * others[-1]
+        width = merge * cores
         pairs = [
-            (team * merge + share, partner * merge + share)
+            (team * width + member, partner * width + member)
             for team, partner in enumerate(partners)
-            for share in range(merge)
+            for member in range(width)
         ]
         others.append(lax.ppermute(sent, "ax", pairs))
     radial_field = pl.pallas_call(
         solve_kernel,
         out_shape=pltpu.VMEM((span, size, radius_count), f32),
-        in_specs=[whole()] * (8 + len(rounds)),
+        in_specs=[whole()] * (11 + len(rounds)),
         out_specs=whole(),
         scratch_shapes=[pltpu.VMEM((span, size, radius_count), f32)] * 2,
         name="solve_and_radial_back",
@@ -359,10 +419,13 @@
         in_vmem(radial_basis),
         in_vmem(decay),
         in_vmem(gain),
+        in_vmem(link),
+        in_vmem(lead),
         in_vmem(mix),
         in_vmem(near),
         in_vmem(ends),
         in_vmem(carries),
+        in_vmem(twin),
         *map(in_vmem, others),
     )
     collected = lax.all_to_all(

time: 86.1 us -> 82 us (0.952)
  blocking collectives: 66.5 us -> 60.7 us
  waiting for transfers between devices: 3.45 us -> 5.55 us
    all_to_all x1, blocking collectives: 18.2 us -> 15.4 us  [body(): lax.all_to_all(spectral, ('plane', 'ax'), 0, 0, tiled=True, axis_index_gr...]
    all_to_all x1, blocking collectives: 16.5 us -> 14.4 us  [body(): lax.all_to_all(radial_field, ('plane', 'ax'), 0, 0, tiled=True, axis_inde...]
    ppermute x0 -> x1, waiting for transfers between devices: none -> 1.24 us  [body(): lax.ppermute(carries, 'ax', [(index, index ^ 1) for index in range(blocks)])]
    all_to_all x1, blocking collectives: 14.6 us -> 13.6 us  [body(): lax.all_to_all(spatial.reshape(planes, local_t, radius_count), 'plane', 0...]
    ppermute x2, waiting for transfers between devices: 3.45 us -> 4.31 us  [body(): others.append(lax.ppermute(sent, 'ax', pairs))]
  transfers between devices with their start and end apart: 2 -> 3, of which waited for: 2 -> 3; matrix products, arithmetic and copies ran while one was open for 0% -> 0% of each run, Pallas kernels for 0% -> 0%
where the time goes in v3:
time: 82 us; the launch traced here: 81.8 us
  blocking collectives  60.7 us (74%)
  starting transfers between devices  8.07 us (10%)
  Pallas kernels  7.33 us (9%)
  waiting for transfers between devices  5.55 us (7%)
    all_to_all x1, blocking collectives, body(): piece = lax.all_to_all(turned, 'plane', 0, 0, tiled=True)  17.3 us
    all_to_all x1, blocking collectives, body(): lax.all_to_all(spectral, ('plane', 'ax'), 0, 0, tiled=True, axis_index_gr...  15.4 us
    all_to_all x1, blocking collectives, body(): lax.all_to_all(radial_field, ('plane', 'ax'), 0, 0, tiled=True, axis_inde...  14.4 us
    all_to_all x1, blocking collectives, body(): lax.all_to_all(spatial.reshape(planes, local_t, radius_count), 'plane', 0...  13.6 us
    ppermute x2, starting transfers between devices, body(): others.append(lax.ppermute(sent, 'ax', pairs))  7.97 us
    ppermute x2, waiting for transfers between devices, body(): others.append(lax.ppermute(sent, 'ax', pairs))  4.31 us
    pallas_call x1, Pallas kernels, body(): pl.pallas_call(prepare_kernel, out_shape=(pltpu.VMEM((depth_cells, local_...  1.94 us
  transfers between devices with their start and end apart: 3, of which 3 were waited for; matrix products, arithmetic and copies ran while one was open for 0% of the time, Pallas kernels for 0%

profile of v3, /device:TPU:8, one launch (start us, length us, event | category | flops | bytes accessed | tf_op | source)
XLA Modules:
  0.0 81.8 jit_solution(2482692689981517032)
XLA Ops:
  0.0 1.9 %cells_first.1 = (f32[16,64,128]{2,1,0:T(8,128)S(1)}, bf16[2,512,1024]{2,1,0:T(8,128)(2,1)S(1)}, f32[32,128]{1,0:T(8,128)S(1)}, f32[32,128]{1,0:T(8,128)S(1)}, f...) custom-call(f32[64,16,128]{2,1,0:T(8,128)} %source_ref.1, ...), custom_call_target="tpu_custom_call" | custom-call | tf_op jit(solution)/shard_map/cells_first/pallas_call | solution.py:349
  2.0 17.3 %all_to_all.20 = f32[16,64,128]{2,1,0:T(8,128)S(1)} all-to-all(f32[16,64,128]{2,1,0:T(8,128)S(1)} %get-tuple-element.17), channel_id=1, replica_groups=mesh['plane'=16,'ax'=16] {'plane'}, dimensions={0} | all-to-all | bytes 1048576 | tf_op jit(solution)/shard_map/all_to_all | solution.py:373
  19.3 0.0 copy-start
  19.3 0.0 copy-start.2
  19.3 1.0 %fourier_forward.1 = f32[32,32,128]{2,1,0:T(8,128)S(1)} custom-call(bf16[2,512,1024]{2,1,0:T(8,128)(2,1)S(1)} %get-tuple-element.16.table_ref, f32[1024,128]{1,0:T(8,128)S(1)} %bitcast.21), custom_call_target="tpu_custom_call" | custom-call | tf_op jit(solution)/shard_map/fourier_forward/pallas_call | solution.py:374
  20.3 15.4 %all_to_all.21.x_ref = f32[32,32,128]{2,1,0:T(8,128)S(1)} all-to-all(f32[32,32,128]{2,1,0:T(8,128)S(1)} %fourier_forward.1), channel_id=1, replica_groups={{0,16,32,48,64,80,96,112,128,144,160,176,192,208,224,240,2,18,34,50,66,..., dimensions={0} | all-to-all | bytes 1048576 | tf_op jit(solution)/shard_map/all_to_all | solution.py:382
  35.7 0.0 copy-done
  35.7 0.0 copy-done.2
  35.7 1.3 %radial_forward.1 = (f32[32,32,128]{2,1,0:T(8,128)S(1)}, f32[2,2,32,128]{3,2,1,0:T(8,128)S(1)}) custom-call(f32[32,32,128]{2,1,0:T(8,128)S(1)} %all_to_all.21.x_ref, f32[64,128,128]{2,1,0:T(8,128)S(1)} %copy-done, f32[1,128]{1,0:T(1,128)S(1)} %bitcast.23, f32[32,128]{1,0:T(8,128)S(1)} %get-tuple-element.18.decay_ref), custom_call_target="tpu_custom_call" | custom-call | tf_op jit(solution)/shard_map/radial_forward/pallas_call | solution.py:385
  36.9 0.1 collective-permute-start
  37.0 1.2 %collective-permute-done.twin_ref = f32[2,2,32,128]{3,2,1,0:T(8,128)S(1)} collective-permute-done((f32[2,2,32,128]{3,2,1,0:T(8,128)S(1)}, f32[2,2,32,128]{3,2,1,0:T(8,128)S(1)}, u32[]{:S(2)}, u32[]{:S(2)}) %collective-permute-start) | collective-permute-done | bytes 65568 | tf_op jit(solution)/shard_map/ppermute | solution.py:396
  38.3 3.4 %collective-permute-start.1 = (f32[2,32,128]{2,1,0:T(8,128)S(1)}, f32[2,32,128]{2,1,0:T(8,128)S(1)}, u32[]{:S(2)}, u32[]{:S(2)}) collective-permute-start(f32[2,32,128]{2,1,0:T(8,128)S(1)} %fusion.1), channel_id=1, source_target_pairs={{0,4},{1,5},{2,6},{3,7},{4,0},{5,1},{6,2},{7,3},{8,12},{9,13},{10,... | collective-permute-start | bytes 98312 | tf_op jit(solution)/shard_map/ppermute | solution.py:408
  41.7 2.4 %collective-permute-done.1.refs_0_ = f32[2,32,128]{2,1,0:T(8,128)S(1)} collective-permute-done((f32[2,32,128]{2,1,0:T(8,128)S(1)}, f32[2,32,128]{2,1,0:T(8,128)S(1)}, u32[]{:S(2)}, u32[]{:S(2)}) %collective-permute-start.1) | collective-permute-done | bytes 32800 | tf_op jit(solution)/shard_map/ppermute | solution.py:408
  44.1 4.6 %collective-permute-start.2 = (f32[2,32,128]{2,1,0:T(8,128)S(1)}, f32[2,32,128]{2,1,0:T(8,128)S(1)}, u32[]{:S(2)}, u32[]{:S(2)}) collective-permute-start(f32[2,32,128]{2,1,0:T(8,128)S(1)} %fusion.2), channel_id=1, source_target_pairs={{0,12},{1,13},{2,14},{3,15},{4,8},{5,9},{6,10},{7,11},{8,4},{9,5},... | collective-permute-start | bytes 98312 | tf_op jit(solution)/shard_map/ppermute | solution.py:408
  48.7 1.9 %collective-permute-done.2.refs_1_ = f32[2,32,128]{2,1,0:T(8,128)S(1)} collective-permute-done((f32[2,32,128]{2,1,0:T(8,128)S(1)}, f32[2,32,128]{2,1,0:T(8,128)S(1)}, u32[]{:S(2)}, u32[]{:S(2)}) %collective-permute-start.2) | collective-permute-done | bytes 32800 | tf_op jit(solution)/shard_map/ppermute | solution.py:408
  50.6 0.0 copy-start.1
  50.6 1.5 %solve_and_radial_back.1 = f32[32,32,128]{2,1,0:T(8,128)S(1)} custom-call(f32[32,32,128]{2,1,0:T(8,128)S(1)} %get-tuple-element.19.f_ref, f32[64,128,128]{2,1,0:T(8,128)S(1)} %copy-done, f32[32,128]{1,0:T(8,128)S(1)} %get-tuple-element.18.decay_ref, f32[32,128]{1,0:T(8,128)S(1)} %get-tuple-element.20.gain_ref, ...), custom_call_target="tpu_custom_call" | custom-call | tf_op jit(solution)/shard_map/solve_and_radial_back/pallas_call | solution.py:409
  52.1 14.4 %all_to_all.22.x_ref = f32[32,32,128]{2,1,0:T(8,128)S(1)} all-to-all(f32[32,32,128]{2,1,0:T(8,128)S(1)} %solve_and_radial_back.1), channel_id=1, replica_groups={{0,16,32,48,64,80,96,112,128,144,160,176,192,208,224,240,2,18,34,50,66,..., dimensions={0} | all-to-all | bytes 1048576 | tf_op jit(solution)/shard_map/all_to_all | solution.py:431
  66.5 0.0 copy-done.1
  66.5 0.7 fourier_backward.1
  67.2 13.6 %all_to_all.23.x_ref = f32[16,64,128]{2,1,0:T(8,128)S(1)} all-to-all(f32[16,64,128]{2,1,0:T(8,128)S(1)} %bitcast.22), channel_id=1, replica_groups=mesh['plane'=16,'ax'=16] {'plane'}, dimensions={0} | all-to-all | bytes 1048576 | tf_op jit(solution)/shard_map/all_to_all | solution.py:442
  80.9 0.9 %angles_first.1 = f32[64,16,128]{2,1,0:T(8,128)} custom-call(f32[16,64,128]{2,1,0:T(8,128)S(1)} %all_to_all.23.x_ref), custom_call_target="tpu_custom_call" | custom-call | tf_op jit(solution)/shard_map/angles_first/pallas_call | solution.py:445
  (2 shorter events, 0.0 us)
Async XLA Ops:
  19.3 16.4 %copy-start = (f32[64,128,128]{2,1,0:T(8,128)S(1)}, f32[64,128,128]{2,1,0:T(8,128)}, u32[]{:S(2)}) copy-start(f32[64,128,128]{2,1,0:T(8,128)} %basis_ref.3) | copy-start | bytes 12582916
  19.3 16.4 %copy-start.2 = (f32[128]{0:T(128)S(1)}, f32[128]{0:T(128)}, u32[]{:S(2)}) copy-start(f32[128]{0:T(128)} %param.8) | copy-start | bytes 1540
  36.9 1.3 %collective-permute-start = (f32[2,2,32,128]{3,2,1,0:T(8,128)S(1)}, f32[2,2,32,128]{3,2,1,0:T(8,128)S(1)}, u32[]{:S(2)}, u32[]{:S(2)}) collective-permute-start(f32[2,2,32,128]{3,2,1,0:T(8,128)S(1)} %get-tuple-element.26.carry_ref), channel_id=1, source_target_pairs={{0,1},{1,0},{2,3},{3,2},{4,5},{5,4},{6,7},{7,6},{8,9},{9,8},{10,11... | collective-permute-start | bytes 196616 | tf_op jit(solution)/shard_map/ppermute | solution.py:396
  38.3 5.8 %collective-permute-start.1 = (f32[2,32,128]{2,1,0:T(8,128)S(1)}, f32[2,32,128]{2,1,0:T(8,128)S(1)}, u32[]{:S(2)}, u32[]{:S(2)}) collective-permute-start(f32[2,32,128]{2,1,0:T(8,128)S(1)} %fusion.1), channel_id=1, source_target_pairs={{0,4},{1,5},{2,6},{3,7},{4,0},{5,1},{6,2},{7,3},{8,12},{9,13},{10,... | collective-permute-start | bytes 98312 | tf_op jit(solution)/shard_map/ppermute | solution.py:408
  44.1 6.5 %collective-permute-start.2 = (f32[2,32,128]{2,1,0:T(8,128)S(1)}, f32[2,32,128]{2,1,0:T(8,128)S(1)}, u32[]{:S(2)}, u32[]{:S(2)}) collective-permute-start(f32[2,32,128]{2,1,0:T(8,128)S(1)} %fusion.2), channel_id=1, source_target_pairs={{0,12},{1,13},{2,14},{3,15},{4,8},{5,9},{6,10},{7,11},{8,4},{9,5},... | collective-permute-start | bytes 98312 | tf_op jit(solution)/shard_map/ppermute | solution.py:408
  50.6 15.9 %copy-start.1 = (bf16[2,512,1024]{2,1,0:T(8,128)(2,1)S(1)}, bf16[2,512,1024]{2,1,0:T(8,128)(2,1)}, u32[]{:S(2)}) copy-start(bf16[2,512,1024]{2,1,0:T(8,128)(2,1)} %constant.7.clone.table_ref) | copy-start | bytes 6291460

commit v4 on v3

--- a/solution.py
+++ b/solution.py
@@ -3,7 +3,6 @@
 
 import jax
 import jax.numpy as jnp
-import ml_dtypes
 import numpy as np
 from jax import lax
 from jax.experimental import pallas as pl
@@ -18,30 +17,31 @@
 compact = pltpu.CompilerParams(vmem_limit_bytes=16 * 2**20)
 
 
-def mode_order(total, planes, share):
+def mode_offset(place, size):
+    quarter = size // 4
+    if place < quarter:
+        return 4 * place
+    if place < 2 * quarter:
+        return 4 * (place - quarter) + 2
+    return 2 * (place - 2 * quarter) + 1
+
+
+def fourier_parts(total, planes, share):
     local = total // planes
     size = local // share
-    share_at, plane_at, parity, half = np.meshgrid(
-        np.arange(share), np.arange(planes), np.arange(2), np.arange(size // 2), indexing="ij"
-    )
-    return plane_at * local + share_at * size + 2 * half + parity
-
-
-def fourier_halves(total, planes, share):
-    order = mode_order(total, planes, share).transpose(2, 0, 1, 3).reshape(2, total // 2)
-    angles = np.arange(total // 2)
-    middle = total // 2
-    harmonic = np.where(order <= middle, order, order - middle)
-    radians = (harmonic[:, :, None] * angles % total) * (2.0 * math.pi / total)
-    factor = np.where((order == 0) | (order == middle), math.sqrt(1.0 / total), math.sqrt(2.0 / total))
-    waves = np.where((order <= middle)[:, :, None], np.cos(radians), np.sin(radians))
-    return (waves * factor[:, :, None]).astype(np.float32)
-
-
-def split_table(table):
-    high = table.astype(ml_dtypes.bfloat16)
-    rest = (table - high.astype(np.float32)).astype(ml_dtypes.bfloat16)
-    return np.concatenate([high, rest], axis=2)
+    bounds = (0, size // 4, size // 2, size)
+    tables = []
+    for which, columns in enumerate((total // 4, total // 4, total // 2)):
+        offsets = np.array([mode_offset(place, size) for place in range(bounds[which], bounds[which + 1])])
+        share_at, plane_at, offset = np.meshgrid(np.arange(share), np.arange(planes), offsets, indexing="ij")
+        order = (plane_at * local + share_at * size + offset).reshape(-1)
+        middle = total // 2
+        harmonic = np.where(order <= middle, order, order - middle)
+        radians = (harmonic[:, None] * np.arange(columns) % total) * (2.0 * math.pi / total)
+        factor = np.where((order == 0) | (order == middle), math.sqrt(1.0 / total), math.sqrt(2.0 / total))
+        waves = np.where((order <= middle)[:, None], np.cos(radians), np.sin(radians))
+        tables.append((waves * factor[:, None]).astype(np.float32))
+    return np.stack(tables[:2]), tables[2][None]
 
 
 def split2(value):
@@ -66,6 +66,13 @@
 
 def twice(value, axis):
     return jnp.concatenate([value, value], axis=axis)
+
+
+def swap_tiles(from_ref, to_ref, firsts, seconds):
+    for first in firsts:
+        for second in seconds:
+            rows, columns = slice(first, first + firsts.step), slice(second, second + seconds.step)
+            to_ref[rows, columns, :] = jnp.swapaxes(from_ref[columns, rows, :], 0, 1)
 
 
 def swaps(teams):
@@ -85,7 +92,7 @@
 
 
 def prepare_kernel(
-    source_ref, shifts_ref, table_ref, out_ref, hold_ref, decay_ref, gain_ref, link_ref, lead_ref, mix_ref, near_ref, end_ref,
+    source_ref, shifts_ref, even_ref, odd_ref, out_ref, even_out_ref, odd_out_ref, decay_ref, gain_ref, link_ref, lead_ref, mix_ref, near_ref, end_ref,
     held_ref, shift_ref, sems, extra_sems,
 ):
     cells, angles, _ = out_ref.shape
@@ -95,7 +102,10 @@
     chunks = sems.shape[0]
     rows = angles // chunks
     shift_copy = pltpu.make_async_copy(shifts_ref, shift_ref, extra_sems.at[0])
-    table_copy = pltpu.make_async_copy(table_ref, hold_ref, extra_sems.at[1])
+    table_copies = [
+        pltpu.make_async_copy(even_ref, even_out_ref, extra_sems.at[1]),
+        pltpu.make_async_copy(odd_ref, odd_out_ref, extra_sems.at[2]),
+    ]
     copies = [
         pltpu.make_async_copy(
             source_ref.at[pl.ds(chunk * rows, rows)], held_ref.at[pl.ds(chunk * rows, rows)], sems.at[chunk]
@@ -105,13 +115,19 @@
     shift_copy.start()
     for copy in copies:
         copy.start()
-    table_copy.start()
+    for copy in table_copies:
+        copy.start()
 
     core, share, team = place_in_team()
     first = share * size
     shift_copy.wait()
     shifts = jnp.concatenate(
-        [shift_ref[pl.ds(first + parity, size // 2, stride=2), :] for parity in range(2)], axis=0
+        [
+            shift_ref[pl.ds(first, size // 4, stride=4), :],
+            shift_ref[pl.ds(first + 2, size // 4, stride=4), :],
+            shift_ref[pl.ds(first + 1, size // 2, stride=2), :],
+        ],
+        axis=0,
     )
     rise = 0.5 * jnp.sqrt((2.0 + shifts) - 2.0)
     cosh_half = jnp.sqrt(1.0 + rise * rise)
@@ -181,10 +197,9 @@
 
     for chunk, copy in enumerate(copies):
         copy.wait()
-        part = pl.ds(chunk * rows, rows)
-        for cell in range(cells):
-            out_ref[cell, part, :] = held_ref[part, cell, :]
-    table_copy.wait()
+        swap_tiles(held_ref, out_ref, range(0, cells, min(8, cells)), range(chunk * rows, (chunk + 1) * rows, min(8, rows)))
+    for copy in table_copies:
+        copy.wait()
 
 
 def place_in_team():
@@ -204,45 +219,63 @@
     return result
 
 
-def forward_kernel(table_ref, x_ref, out_ref):
-    half_t = x_ref.shape[0] // 2
-    width = x_ref.shape[1]
+def forward_kernel(even_ref, odd_ref, x_ref, out_ref):
+    total, width = x_ref.shape
     blocks, size, _ = out_ref.shape
-    low, high = x_ref[:half_t], x_ref[half_t:]
-    for parity in range(2):
-        folded = low + high if parity == 0 else low - high
+    half, quarter = total // 2, total // 4
+    low, high = x_ref[:half], x_ref[half:]
+    kept, turned = low + high, low - high
+    parts = (
+        (even_ref, 0, kept[:quarter] + kept[quarter:]),
+        (even_ref, 1, kept[:quarter] - kept[quarter:]),
+        (odd_ref, 0, turned),
+    )
+    at = 0
+    for table_ref, which, folded in parts:
+        rows = table_ref.shape[1] // blocks
         a, b, c = split3(folded)
-        first = mul(table_ref[parity], twice(jnp.concatenate([a, b], axis=1), 0))
-        result = first[:, :width] + (first[:, width:] + mul(table_ref[parity, :, :half_t], c))
-        out_ref[:, parity * (size // 2) : (parity + 1) * (size // 2), :] = result.reshape(
-            blocks, size // 2, width
-        )
-
-
-def backward_kernel(table_ref, x_ref, out_ref):
+        leading, rest = split2(table_ref[which])
+        pair = jnp.concatenate([a, b], axis=1)
+        first = mul(leading, pair) + mul(rest, pair)
+        result = first[:, :width] + (first[:, width:] + mul(leading, c))
+        out_ref[:, at : at + rows, :] = result.reshape(blocks, rows, width)
+        at += rows
+
+
+def backward_kernel(even_ref, odd_ref, x_ref, out_ref):
     blocks, size, width = x_ref.shape
-    half_k = blocks * size // 2
+    total = out_ref.shape[0]
+    half, quarter = total // 2, total // 4
     sums = []
-    for parity in range(2):
-        part = x_ref[:, parity * (size // 2) : (parity + 1) * (size // 2), :].reshape(-1, width)
-        a, b = split2(part)
-        first = mul(table_ref[parity, :, :half_k], jnp.concatenate([a, b], axis=1))
-        sums.append(first[:, :width] + (first[:, width:] + mul(table_ref[parity, :, half_k:], a)))
-    half_t = out_ref.shape[0] // 2
-    out_ref[:half_t] = sums[0] + sums[1]
-    out_ref[half_t:] = sums[0] - sums[1]
+    at = 0
+    for table_ref, which in ((even_ref, 0), (even_ref, 1), (odd_ref, 0)):
+        rows = table_ref.shape[2] // blocks
+        a, b = split2(x_ref[:, at : at + rows, :].reshape(rows * blocks, width))
+        leading, rest = split2(table_ref[which])
+        first = mul(leading, jnp.concatenate([a, b], axis=1))
+        sums.append(first[:, :width] + (first[:, width:] + mul(rest, a)))
+        at += rows
+    fours, twos, odd = sums
+    for which, even in enumerate((fours + twos, fours - twos)):
+        part = odd[which * quarter : (which + 1) * quarter]
+        out_ref[which * quarter : (which + 1) * quarter] = even + part
+        out_ref[half + which * quarter : half + (which + 1) * quarter] = even - part
 
 
 def modal_kernel(x_ref, basis_ref, weights_ref, decay_ref, f_ref, carry_ref):
     depth, size, _ = x_ref.shape
     weights = weights_ref[...]
     first = place_in_team()[1] * size
-    for place in range(size):
-        parity, half = divmod(place, size // 2)
-        values = jnp.concatenate(split3(x_ref[:, place, :] * weights), axis=0)
-        basis = jnp.concatenate(split2(basis_ref[first + (2 * half + parity)]), axis=0)
-        result = mul(twice(values, 1), basis)
-        f_ref[:, place, :] = result[:depth] + (result[depth : 2 * depth] + result[2 * depth :])
+    tile = min(8, size)
+    for group in range(0, size, tile):
+        rows = jnp.swapaxes(x_ref[:, group : group + tile, :] * weights, 0, 1)
+        results = []
+        for inner in range(tile):
+            values = jnp.concatenate(split3(rows[inner]), axis=0)
+            basis = jnp.concatenate(split2(basis_ref[first + mode_offset(group + inner, size)]), axis=0)
+            result = mul(twice(values, 1), basis)
+            results.append(result[:depth] + (result[depth : 2 * depth] + result[2 * depth :]))
+        f_ref[:, group : group + tile, :] = jnp.swapaxes(jnp.stack(results), 0, 1)
     decay = decay_ref[...]
     part = depth // merge
     ups = [f_ref[which * part] for which in range(merge)]
@@ -292,23 +325,30 @@
             ups[which] = ups[which] + f_ref[low]
             downs[which] = downs[which] * decay + f_ref[high]
             down_ref[high] = downs[which]
-    for place in range(size):
-        parity, half = divmod(place, size // 2)
-        field = (up_ref[:, place, :] + down_ref[:, place, :]) * gain_ref[place : place + 1, :]
-        values = jnp.concatenate(split2(field), axis=0)
-        basis = jnp.concatenate(split2(basis_ref[first + (2 * half + parity)]), axis=1)
-        result = mul_t(twice(values, 1), basis)
-        out_ref[:, place, :] = result[:depth] + result[depth:]
-
-
-def scatter_kernel(x_ref, out_ref, row_sems):
-    rows = [
-        pltpu.make_async_copy(x_ref.at[cell], out_ref.at[:, cell], row_sems.at[cell])
-        for cell in range(x_ref.shape[0])
-    ]
-    for copy in rows:
-        copy.start()
-    for copy in rows:
+    tile = min(8, size)
+    for group in range(0, size, tile):
+        part = slice(group, group + tile)
+        rows = jnp.swapaxes((up_ref[:, part, :] + down_ref[:, part, :]) * gain_ref[part, :], 0, 1)
+        results = []
+        for inner in range(tile):
+            values = jnp.concatenate(split2(rows[inner]), axis=0)
+            basis = jnp.concatenate(split2(basis_ref[first + mode_offset(group + inner, size)]), axis=1)
+            result = mul_t(twice(values, 1), basis)
+            results.append(result[:depth] + result[depth:])
+        out_ref[:, part, :] = jnp.swapaxes(jnp.stack(results), 0, 1)
+
+
+def scatter_kernel(x_ref, out_ref, turned_ref, sems):
+    cells, angles, _ = x_ref.shape
+    chunks = sems.shape[0]
+    rows = angles // chunks
+    copies = []
+    for chunk in range(chunks):
+        swap_tiles(x_ref, turned_ref, range(chunk * rows, (chunk + 1) * rows, min(8, rows)), range(0, cells, min(8, cells)))
+        part = pl.ds(chunk * rows, rows)
+        copies.append(pltpu.make_async_copy(turned_ref.at[part], out_ref.at[part], sems.at[chunk]))
+        copies[-1].start()
+    for copy in copies:
         copy.wait()
 
 
@@ -332,9 +372,9 @@
     size = local_t // merge
     span = depth_cells * merge
     teams = blocks // (merge * cores)
-    table = fourier_halves(total_t, planes, merge)
-    forward_table = jnp.asarray(split_table(table))
-    backward_table = jnp.asarray(split_table(table.transpose(0, 2, 1)))
+    tables = fourier_parts(total_t, planes, merge)
+    forward_tables = [jnp.asarray(table) for table in tables]
+    backward_tables = [jnp.asarray(table.transpose(0, 2, 1)) for table in tables]
     neighbours = [
         [
             plane * blocks + (team * merge + share) * cores + core
@@ -346,11 +386,11 @@
     ]
     rounds = swaps(teams)
 
-    turned, held_table, decay, gain, link, lead, mix, near, ends = pl.pallas_call(
+    turned, held_even, held_odd, decay, gain, link, lead, mix, near, ends = pl.pallas_call(
         prepare_kernel,
         out_shape=(
             pltpu.VMEM((depth_cells, local_t, radius_count), f32),
-            pltpu.VMEM(forward_table.shape, bf16),
+            *(pltpu.VMEM(table.shape, f32) for table in forward_tables),
             pltpu.VMEM((size, radius_count), f32),
             pltpu.VMEM((size, radius_count), f32),
             pltpu.VMEM((2, merge + 1, merge, 2, size, radius_count), f32),
@@ -359,26 +399,26 @@
             pltpu.VMEM((len(rounds), 2, size, radius_count), f32),
             pltpu.VMEM((2, 2, size, radius_count), f32),
         ),
-        in_specs=[whole(pltpu.HBM)] * 3,
-        out_specs=(whole(),) * 9,
+        in_specs=[whole(pltpu.HBM)] * 4,
+        out_specs=(whole(),) * 10,
         scratch_shapes=[
             pltpu.VMEM(source.shape, f32),
             pltpu.VMEM(mode_shifts.shape, f32),
-            pltpu.SemaphoreType.DMA((4,)),
             pltpu.SemaphoreType.DMA((2,)),
+            pltpu.SemaphoreType.DMA((3,)),
         ],
         name="cells_first",
         compiler_params=compact,
-    )(in_hbm(source), in_hbm(mode_shifts), in_hbm(forward_table))
+    )(in_hbm(source), in_hbm(mode_shifts), *map(in_hbm, forward_tables))
     piece = lax.all_to_all(turned, "plane", 0, 0, tiled=True)
     spectral = pl.pallas_call(
         forward_kernel,
         out_shape=pltpu.VMEM((planes * merge, size, radius_count), f32),
-        in_specs=[whole()] * 2,
+        in_specs=[whole()] * 3,
         out_specs=whole(),
         name="fourier_forward",
         compiler_params=compact,
-    )(in_vmem(held_table), in_vmem(piece.reshape(total_t, radius_count)))
+    )(in_vmem(held_even), in_vmem(held_odd), in_vmem(piece.reshape(total_t, radius_count)))
     modal = lax.all_to_all(
         spectral, ("plane", "ax"), 0, 0, tiled=True, axis_index_groups=neighbours
     )
@@ -434,11 +474,11 @@
     spatial = pl.pallas_call(
         backward_kernel,
         out_shape=pltpu.VMEM((total_t, radius_count), f32),
-        in_specs=[whole()] * 2,
+        in_specs=[whole()] * 3,
         out_specs=whole(),
         name="fourier_backward",
         compiler_params=compact,
-    )(in_vmem(backward_table), in_vmem(collected))
+    )(*map(in_vmem, backward_tables), in_vmem(collected))
     pressure = lax.all_to_all(
         spatial.reshape(planes, local_t, radius_count), "plane", 0, 0, tiled=True
     )
@@ -447,7 +487,7 @@
         out_shape=jax.ShapeDtypeStruct(source.shape, f32),
         in_specs=[whole()],
         out_specs=whole(pltpu.HBM),
-        scratch_shapes=[pltpu.SemaphoreType.DMA((depth_cells,))],
+        scratch_shapes=[pltpu.VMEM(source.shape, f32), pltpu.SemaphoreType.DMA((4,))],
         name="angles_first",
         compiler_params=compact,
     )(in_vmem(pressure))

time: 82 us -> 80.5 us (0.982)
  Pallas kernels: 7.33 us -> 5.87 us
where the time goes in v4:
time: 80.5 us; the launch traced here: 80.3 us
  blocking collectives  60.7 us (75%)
  starting transfers between devices  8.07 us (10%)
  Pallas kernels  5.87 us (7%)
  waiting for transfers between devices  5.55 us (7%)
    all_to_all x1, blocking collectives, body(): piece = lax.all_to_all(turned, 'plane', 0, 0, tiled=True)  17.4 us
    all_to_all x1, blocking collectives, body(): lax.all_to_all(spectral, ('plane', 'ax'), 0, 0, tiled=True, axis_index_gr...  15.3 us
    all_to_all x1, blocking collectives, body(): lax.all_to_all(radial_field, ('plane', 'ax'), 0, 0, tiled=True, axis_inde...  14.4 us
    all_to_all x1, blocking collectives, body(): lax.all_to_all(spatial.reshape(planes, local_t, radius_count), 'plane', 0...  13.6 us
    ppermute x2, starting transfers between devices, body(): others.append(lax.ppermute(sent, 'ax', pairs))  7.97 us
    ppermute x2, waiting for transfers between devices, body(): others.append(lax.ppermute(sent, 'ax', pairs))  4.31 us
    pallas_call x1, Pallas kernels, body(): pl.pallas_call(prepare_kernel, out_shape=(pltpu.VMEM((depth_cells, local_...  1.75 us
  transfers between devices with their start and end apart: 3, of which 3 were waited for; matrix products, arithmetic and copies ran while one was open for 0% of the time, Pallas kernels for 0%

profile of v4, /device:TPU:8, one launch (start us, length us, event | category | flops | bytes accessed | tf_op | source)
XLA Modules:
  0.0 80.3 jit_solution(6049529195541886009)
XLA Ops:
  0.0 0.0 copy-start
  0.0 0.0 copy-start.3
  0.0 1.8 %cells_first.1 = (f32[16,64,128]{2,1,0:T(8,128)S(1)}, f32[2,256,256]{2,1,0:T(8,128)S(1)}, f32[1,512,512]{2,1,0:T(8,128)S(1)}, f32[32,128]{1,0:T(8,128)S(1)}, f32...) custom-call(f32[64,16,128]{2,1,0:T(8,128)} %source_ref.1, ...), custom_call_target="tpu_custom_call" | custom-call | tf_op jit(solution)/shard_map/cells_first/pallas_call | solution.py:389
  1.8 17.4 %all_to_all.20 = f32[16,64,128]{2,1,0:T(8,128)S(1)} all-to-all(f32[16,64,128]{2,1,0:T(8,128)S(1)} %get-tuple-element.19), channel_id=1, replica_groups=mesh['plane'=16,'ax'=16] {'plane'}, dimensions={0} | all-to-all | bytes 1048576 | tf_op jit(solution)/shard_map/all_to_all | solution.py:413
  19.2 0.8 %fourier_forward.1 = f32[32,32,128]{2,1,0:T(8,128)S(1)} custom-call(f32[2,256,256]{2,1,0:T(8,128)S(1)} %get-tuple-element.17.even_ref, f32[1,512,512]{2,1,0:T(8,128)S(1)} %get-tuple-element.18.odd_ref, f32[1024,128]{1,0:T(8,128)S(1)} %bitcast.21), custom_call_target="tpu_custom_call" | custom-call | tf_op jit(solution)/shard_map/fourier_forward/pallas_call | solution.py:414
  20.0 15.3 %all_to_all.21.x_ref = f32[32,32,128]{2,1,0:T(8,128)S(1)} all-to-all(f32[32,32,128]{2,1,0:T(8,128)S(1)} %fourier_forward.1), channel_id=1, replica_groups={{0,16,32,48,64,80,96,112,128,144,160,176,192,208,224,240,2,18,34,50,66,..., dimensions={0} | all-to-all | bytes 1048576 | tf_op jit(solution)/shard_map/all_to_all | solution.py:422
  35.3 0.0 copy-done
  35.3 0.0 copy-done.3
  35.3 0.9 %radial_forward.1 = (f32[32,32,128]{2,1,0:T(8,128)S(1)}, f32[2,2,32,128]{3,2,1,0:T(8,128)S(1)}) custom-call(f32[32,32,128]{2,1,0:T(8,128)S(1)} %all_to_all.21.x_ref, f32[64,128,128]{2,1,0:T(8,128)S(1)} %copy-done, f32[1,128]{1,0:T(1,128)S(1)} %bitcast.23, f32[32,128]{1,0:T(8,128)S(1)} %get-tuple-element.20.decay_ref), custom_call_target="tpu_custom_call" | custom-call | tf_op jit(solution)/shard_map/radial_forward/pallas_call | solution.py:425
  36.2 0.0 copy-start.1
  36.2 0.0 copy-start.2
  36.2 0.1 collective-permute-start
  36.3 1.2 %collective-permute-done.twin_ref = f32[2,2,32,128]{3,2,1,0:T(8,128)S(1)} collective-permute-done((f32[2,2,32,128]{3,2,1,0:T(8,128)S(1)}, f32[2,2,32,128]{3,2,1,0:T(8,128)S(1)}, u32[]{:S(2)}, u32[]{:S(2)}) %collective-permute-start) | collective-permute-done | bytes 65568 | tf_op jit(solution)/shard_map/ppermute | solution.py:436
  37.6 3.4 %collective-permute-start.1 = (f32[2,32,128]{2,1,0:T(8,128)S(1)}, f32[2,32,128]{2,1,0:T(8,128)S(1)}, u32[]{:S(2)}, u32[]{:S(2)}) collective-permute-start(f32[2,32,128]{2,1,0:T(8,128)S(1)} %fusion.1), channel_id=1, source_target_pairs={{0,4},{1,5},{2,6},{3,7},{4,0},{5,1},{6,2},{7,3},{8,12},{9,13},{10,... | collective-permute-start | bytes 98312 | tf_op jit(solution)/shard_map/ppermute | solution.py:448
  40.9 2.4 %collective-permute-done.1.refs_0_ = f32[2,32,128]{2,1,0:T(8,128)S(1)} collective-permute-done((f32[2,32,128]{2,1,0:T(8,128)S(1)}, f32[2,32,128]{2,1,0:T(8,128)S(1)}, u32[]{:S(2)}, u32[]{:S(2)}) %collective-permute-start.1) | collective-permute-done | bytes 32800 | tf_op jit(solution)/shard_map/ppermute | solution.py:448
  43.4 4.6 %collective-permute-start.2 = (f32[2,32,128]{2,1,0:T(8,128)S(1)}, f32[2,32,128]{2,1,0:T(8,128)S(1)}, u32[]{:S(2)}, u32[]{:S(2)}) collective-permute-start(f32[2,32,128]{2,1,0:T(8,128)S(1)} %fusion.2), channel_id=1, source_target_pairs={{0,12},{1,13},{2,14},{3,15},{4,8},{5,9},{6,10},{7,11},{8,4},{9,5},... | collective-permute-start | bytes 98312 | tf_op jit(solution)/shard_map/ppermute | solution.py:448
  48.0 1.9 %collective-permute-done.2.refs_1_ = f32[2,32,128]{2,1,0:T(8,128)S(1)} collective-permute-done((f32[2,32,128]{2,1,0:T(8,128)S(1)}, f32[2,32,128]{2,1,0:T(8,128)S(1)}, u32[]{:S(2)}, u32[]{:S(2)}) %collective-permute-start.2) | collective-permute-done | bytes 32800 | tf_op jit(solution)/shard_map/ppermute | solution.py:448
  49.9 1.0 %solve_and_radial_back.1 = f32[32,32,128]{2,1,0:T(8,128)S(1)} custom-call(f32[32,32,128]{2,1,0:T(8,128)S(1)} %get-tuple-element.21.f_ref, f32[64,128,128]{2,1,0:T(8,128)S(1)} %copy-done, f32[32,128]{1,0:T(8,128)S(1)} %get-tuple-element.20.decay_ref, f32[32,128]{1,0:T(8,128)S(1)} %get-tuple-element.22.gain_ref, ...), custom_call_target="tpu_custom_call" | custom-call | tf_op jit(solution)/shard_map/solve_and_radial_back/pallas_call | solution.py:449
  50.9 14.4 %all_to_all.22.x_ref = f32[32,32,128]{2,1,0:T(8,128)S(1)} all-to-all(f32[32,32,128]{2,1,0:T(8,128)S(1)} %solve_and_radial_back.1), channel_id=1, replica_groups={{0,16,32,48,64,80,96,112,128,144,160,176,192,208,224,240,2,18,34,50,66,..., dimensions={0} | all-to-all | bytes 1048576 | tf_op jit(solution)/shard_map/all_to_all | solution.py:471
  65.3 0.0 copy-done.1
  65.3 0.0 copy-done.2
  65.3 0.6 fourier_backward.1
  65.9 13.6 %all_to_all.23.x_ref = f32[16,64,128]{2,1,0:T(8,128)S(1)} all-to-all(f32[16,64,128]{2,1,0:T(8,128)S(1)} %bitcast.22), channel_id=1, replica_groups=mesh['plane'=16,'ax'=16] {'plane'}, dimensions={0} | all-to-all | bytes 1048576 | tf_op jit(solution)/shard_map/all_to_all | solution.py:482
  79.5 0.8 %angles_first.1 = f32[64,16,128]{2,1,0:T(8,128)} custom-call(f32[16,64,128]{2,1,0:T(8,128)S(1)} %all_to_all.23.x_ref), custom_call_target="tpu_custom_call" | custom-call | tf_op jit(solution)/shard_map/angles_first/pallas_call | solution.py:485
  (2 shorter events, 0.0 us)
Async XLA Ops:
  0.0 35.3 %copy-start = (f32[64,128,128]{2,1,0:T(8,128)S(1)}, f32[64,128,128]{2,1,0:T(8,128)}, u32[]{:S(2)}) copy-start(f32[64,128,128]{2,1,0:T(8,128)} %basis_ref.3) | copy-start | bytes 12582916
  0.0 35.3 %copy-start.3 = (f32[128]{0:T(128)S(1)}, f32[128]{0:T(128)}, u32[]{:S(2)}) copy-start(f32[128]{0:T(128)} %param.10) | copy-start | bytes 1540
  36.2 29.1 %copy-start.1 = (f32[1,512,512]{2,1,0:T(8,128)S(1)}, f32[1,512,512]{2,1,0:T(8,128)}, u32[]{:S(2)}) copy-start(f32[1,512,512]{2,1,0:T(8,128)} %constant.13.clone.odd_ref) | copy-start | bytes 3145732
  36.2 29.1 %copy-start.2 = (f32[2,256,256]{2,1,0:T(8,128)S(1)}, f32[2,256,256]{2,1,0:T(8,128)}, u32[]{:S(2)}) copy-start(f32[2,256,256]{2,1,0:T(8,128)} %constant.12.clone.even_ref) | copy-start | bytes 1572868
  36.2 1.3 %collective-permute-start = (f32[2,2,32,128]{3,2,1,0:T(8,128)S(1)}, f32[2,2,32,128]{3,2,1,0:T(8,128)S(1)}, u32[]{:S(2)}, u32[]{:S(2)}) collective-permute-start(f32[2,2,32,128]{3,2,1,0:T(8,128)S(1)} %get-tuple-element.28.carry_ref), channel_id=1, source_target_pairs={{0,1},{1,0},{2,3},{3,2},{4,5},{5,4},{6,7},{7,6},{8,9},{9,8},{10,11... | collective-permute-start | bytes 196616 | tf_op jit(solution)/shard_map/ppermute | solution.py:436
  37.6 5.8 %collective-permute-start.1 = (f32[2,32,128]{2,1,0:T(8,128)S(1)}, f32[2,32,128]{2,1,0:T(8,128)S(1)}, u32[]{:S(2)}, u32[]{:S(2)}) collective-permute-start(f32[2,32,128]{2,1,0:T(8,128)S(1)} %fusion.1), channel_id=1, source_target_pairs={{0,4},{1,5},{2,6},{3,7},{4,0},{5,1},{6,2},{7,3},{8,12},{9,13},{10,... | collective-permute-start | bytes 98312 | tf_op jit(solution)/shard_map/ppermute | solution.py:448
  43.4 6.5 %collective-permute-start.2 = (f32[2,32,128]{2,1,0:T(8,128)S(1)}, f32[2,32,128]{2,1,0:T(8,128)S(1)}, u32[]{:S(2)}, u32[]{:S(2)}) collective-permute-start(f32[2,32,128]{2,1,0:T(8,128)S(1)} %fusion.2), channel_id=1, source_target_pairs={{0,12},{1,13},{2,14},{3,15},{4,8},{5,9},{6,10},{7,11},{8,4},{9,5},... | collective-permute-start | bytes 98312 | tf_op jit(solution)/shard_map/ppermute | solution.py:448

commit v5 on v4

--- a/solution.py
+++ b/solution.py
@@ -101,7 +101,9 @@
     teams = 2**rounds
     chunks = sems.shape[0]
     rows = angles // chunks
-    shift_copy = pltpu.make_async_copy(shifts_ref, shift_ref, extra_sems.at[0])
+    shift_copy = pltpu.make_async_copy(
+        shifts_ref, shift_ref.at[pl.ds(0, shifts_ref.shape[0])], extra_sems.at[0]
+    )
     table_copies = [
         pltpu.make_async_copy(even_ref, even_out_ref, extra_sems.at[1]),
         pltpu.make_async_copy(odd_ref, odd_out_ref, extra_sems.at[2]),
@@ -403,7 +405,7 @@
         out_specs=(whole(),) * 10,
         scratch_shapes=[
             pltpu.VMEM(source.shape, f32),
-            pltpu.VMEM(mode_shifts.shape, f32),
+            pltpu.VMEM((local_t + 8, radius_count), f32),
             pltpu.SemaphoreType.DMA((2,)),
             pltpu.SemaphoreType.DMA((3,)),
         ],

time: 80.5 us -> 80.5 us (level)
  no operation moved by 1% of the time
where the time goes in v5:
time: 80.5 us; the launch traced here: 80.3 us
  blocking collectives  60.7 us (75%)
  starting transfers between devices  8.07 us (10%)
  Pallas kernels  5.87 us (7%)
  waiting for transfers between devices  5.55 us (7%)
    all_to_all x1, blocking collectives, body(): piece = lax.all_to_all(turned, 'plane', 0, 0, tiled=True)  17.4 us
    all_to_all x1, blocking collectives, body(): lax.all_to_all(spectral, ('plane', 'ax'), 0, 0, tiled=True, axis_index_gr...  15.3 us
    all_to_all x1, blocking collectives, body(): lax.all_to_all(radial_field, ('plane', 'ax'), 0, 0, tiled=True, axis_inde...  14.4 us
    all_to_all x1, blocking collectives, body(): lax.all_to_all(spatial.reshape(planes, local_t, radius_count), 'plane', 0...  13.6 us
    ppermute x2, starting transfers between devices, body(): others.append(lax.ppermute(sent, 'ax', pairs))  7.97 us
    ppermute x2, waiting for transfers between devices, body(): others.append(lax.ppermute(sent, 'ax', pairs))  4.31 us
    pallas_call x1, Pallas kernels, body(): pl.pallas_call(prepare_kernel, out_shape=(pltpu.VMEM((depth_cells, local_...  1.75 us
  transfers between devices with their start and end apart: 3, of which 3 were waited for; matrix products, arithmetic and copies ran while one was open for 0% of the time, Pallas kernels for 0%

profile of v5, /device:TPU:8, one launch (start us, length us, event | category | flops | bytes accessed | tf_op | source)
XLA Modules:
  0.0 80.3 jit_solution(6049529195541886009)
XLA Ops:
  0.0 0.0 copy-start
  0.0 0.0 copy-start.3
  0.0 1.8 %cells_first.1 = (f32[16,64,128]{2,1,0:T(8,128)S(1)}, f32[2,256,256]{2,1,0:T(8,128)S(1)}, f32[1,512,512]{2,1,0:T(8,128)S(1)}, f32[32,128]{1,0:T(8,128)S(1)}, f32...) custom-call(f32[64,16,128]{2,1,0:T(8,128)} %source_ref.1, ...), custom_call_target="tpu_custom_call" | custom-call | tf_op jit(solution)/shard_map/cells_first/pallas_call | solution.py:391
  1.8 17.4 %all_to_all.20 = f32[16,64,128]{2,1,0:T(8,128)S(1)} all-to-all(f32[16,64,128]{2,1,0:T(8,128)S(1)} %get-tuple-element.19), channel_id=1, replica_groups=mesh['plane'=16,'ax'=16] {'plane'}, dimensions={0} | all-to-all | bytes 1048576 | tf_op jit(solution)/shard_map/all_to_all | solution.py:415
  19.2 0.8 %fourier_forward.1 = f32[32,32,128]{2,1,0:T(8,128)S(1)} custom-call(f32[2,256,256]{2,1,0:T(8,128)S(1)} %get-tuple-element.17.even_ref, f32[1,512,512]{2,1,0:T(8,128)S(1)} %get-tuple-element.18.odd_ref, f32[1024,128]{1,0:T(8,128)S(1)} %bitcast.21), custom_call_target="tpu_custom_call" | custom-call | tf_op jit(solution)/shard_map/fourier_forward/pallas_call | solution.py:416
  20.0 15.3 %all_to_all.21.x_ref = f32[32,32,128]{2,1,0:T(8,128)S(1)} all-to-all(f32[32,32,128]{2,1,0:T(8,128)S(1)} %fourier_forward.1), channel_id=1, replica_groups={{0,16,32,48,64,80,96,112,128,144,160,176,192,208,224,240,2,18,34,50,66,..., dimensions={0} | all-to-all | bytes 1048576 | tf_op jit(solution)/shard_map/all_to_all | solution.py:424
  35.3 0.0 copy-done
  35.3 0.0 copy-done.3
  35.3 0.9 %radial_forward.1 = (f32[32,32,128]{2,1,0:T(8,128)S(1)}, f32[2,2,32,128]{3,2,1,0:T(8,128)S(1)}) custom-call(f32[32,32,128]{2,1,0:T(8,128)S(1)} %all_to_all.21.x_ref, f32[64,128,128]{2,1,0:T(8,128)S(1)} %copy-done, f32[1,128]{1,0:T(1,128)S(1)} %bitcast.23, f32[32,128]{1,0:T(8,128)S(1)} %get-tuple-element.20.decay_ref), custom_call_target="tpu_custom_call" | custom-call | tf_op jit(solution)/shard_map/radial_forward/pallas_call | solution.py:427
  36.2 0.0 copy-start.1
  36.2 0.0 copy-start.2
  36.2 0.1 collective-permute-start
  36.3 1.2 %collective-permute-done.twin_ref = f32[2,2,32,128]{3,2,1,0:T(8,128)S(1)} collective-permute-done((f32[2,2,32,128]{3,2,1,0:T(8,128)S(1)}, f32[2,2,32,128]{3,2,1,0:T(8,128)S(1)}, u32[]{:S(2)}, u32[]{:S(2)}) %collective-permute-start) | collective-permute-done | bytes 65568 | tf_op jit(solution)/shard_map/ppermute | solution.py:438
  37.6 3.4 %collective-permute-start.1 = (f32[2,32,128]{2,1,0:T(8,128)S(1)}, f32[2,32,128]{2,1,0:T(8,128)S(1)}, u32[]{:S(2)}, u32[]{:S(2)}) collective-permute-start(f32[2,32,128]{2,1,0:T(8,128)S(1)} %fusion.1), channel_id=1, source_target_pairs={{0,4},{1,5},{2,6},{3,7},{4,0},{5,1},{6,2},{7,3},{8,12},{9,13},{10,... | collective-permute-start | bytes 98312 | tf_op jit(solution)/shard_map/ppermute | solution.py:450
  40.9 2.4 %collective-permute-done.1.refs_0_ = f32[2,32,128]{2,1,0:T(8,128)S(1)} collective-permute-done((f32[2,32,128]{2,1,0:T(8,128)S(1)}, f32[2,32,128]{2,1,0:T(8,128)S(1)}, u32[]{:S(2)}, u32[]{:S(2)}) %collective-permute-start.1) | collective-permute-done | bytes 32800 | tf_op jit(solution)/shard_map/ppermute | solution.py:450
  43.4 4.6 %collective-permute-start.2 = (f32[2,32,128]{2,1,0:T(8,128)S(1)}, f32[2,32,128]{2,1,0:T(8,128)S(1)}, u32[]{:S(2)}, u32[]{:S(2)}) collective-permute-start(f32[2,32,128]{2,1,0:T(8,128)S(1)} %fusion.2), channel_id=1, source_target_pairs={{0,12},{1,13},{2,14},{3,15},{4,8},{5,9},{6,10},{7,11},{8,4},{9,5},... | collective-permute-start | bytes 98312 | tf_op jit(solution)/shard_map/ppermute | solution.py:450
  48.0 1.9 %collective-permute-done.2.refs_1_ = f32[2,32,128]{2,1,0:T(8,128)S(1)} collective-permute-done((f32[2,32,128]{2,1,0:T(8,128)S(1)}, f32[2,32,128]{2,1,0:T(8,128)S(1)}, u32[]{:S(2)}, u32[]{:S(2)}) %collective-permute-start.2) | collective-permute-done | bytes 32800 | tf_op jit(solution)/shard_map/ppermute | solution.py:450
  49.9 1.0 %solve_and_radial_back.1 = f32[32,32,128]{2,1,0:T(8,128)S(1)} custom-call(f32[32,32,128]{2,1,0:T(8,128)S(1)} %get-tuple-element.21.f_ref, f32[64,128,128]{2,1,0:T(8,128)S(1)} %copy-done, f32[32,128]{1,0:T(8,128)S(1)} %get-tuple-element.20.decay_ref, f32[32,128]{1,0:T(8,128)S(1)} %get-tuple-element.22.gain_ref, ...), custom_call_target="tpu_custom_call" | custom-call | tf_op jit(solution)/shard_map/solve_and_radial_back/pallas_call | solution.py:451
  50.9 14.4 %all_to_all.22.x_ref = f32[32,32,128]{2,1,0:T(8,128)S(1)} all-to-all(f32[32,32,128]{2,1,0:T(8,128)S(1)} %solve_and_radial_back.1), channel_id=1, replica_groups={{0,16,32,48,64,80,96,112,128,144,160,176,192,208,224,240,2,18,34,50,66,..., dimensions={0} | all-to-all | bytes 1048576 | tf_op jit(solution)/shard_map/all_to_all | solution.py:473
  65.3 0.0 copy-done.1
  65.3 0.0 copy-done.2
  65.3 0.6 fourier_backward.1
  65.9 13.6 %all_to_all.23.x_ref = f32[16,64,128]{2,1,0:T(8,128)S(1)} all-to-all(f32[16,64,128]{2,1,0:T(8,128)S(1)} %bitcast.22), channel_id=1, replica_groups=mesh['plane'=16,'ax'=16] {'plane'}, dimensions={0} | all-to-all | bytes 1048576 | tf_op jit(solution)/shard_map/all_to_all | solution.py:484
  79.5 0.8 %angles_first.1 = f32[64,16,128]{2,1,0:T(8,128)} custom-call(f32[16,64,128]{2,1,0:T(8,128)S(1)} %all_to_all.23.x_ref), custom_call_target="tpu_custom_call" | custom-call | tf_op jit(solution)/shard_map/angles_first/pallas_call | solution.py:487
  (2 shorter events, 0.0 us)
Async XLA Ops:
  0.0 35.3 %copy-start = (f32[64,128,128]{2,1,0:T(8,128)S(1)}, f32[64,128,128]{2,1,0:T(8,128)}, u32[]{:S(2)}) copy-start(f32[64,128,128]{2,1,0:T(8,128)} %basis_ref.3) | copy-start | bytes 12582916
  0.0 35.3 %copy-start.3 = (f32[128]{0:T(128)S(1)}, f32[128]{0:T(128)}, u32[]{:S(2)}) copy-start(f32[128]{0:T(128)} %param.10) | copy-start | bytes 1540
  36.2 29.1 %copy-start.1 = (f32[1,512,512]{2,1,0:T(8,128)S(1)}, f32[1,512,512]{2,1,0:T(8,128)}, u32[]{:S(2)}) copy-start(f32[1,512,512]{2,1,0:T(8,128)} %constant.13.clone.odd_ref) | copy-start | bytes 3145732
  36.2 29.1 %copy-start.2 = (f32[2,256,256]{2,1,0:T(8,128)S(1)}, f32[2,256,256]{2,1,0:T(8,128)}, u32[]{:S(2)}) copy-start(f32[2,256,256]{2,1,0:T(8,128)} %constant.12.clone.even_ref) | copy-start | bytes 1572868
  36.2 1.3 %collective-permute-start = (f32[2,2,32,128]{3,2,1,0:T(8,128)S(1)}, f32[2,2,32,128]{3,2,1,0:T(8,128)S(1)}, u32[]{:S(2)}, u32[]{:S(2)}) collective-permute-start(f32[2,2,32,128]{3,2,1,0:T(8,128)S(1)} %get-tuple-element.28.carry_ref), channel_id=1, source_target_pairs={{0,1},{1,0},{2,3},{3,2},{4,5},{5,4},{6,7},{7,6},{8,9},{9,8},{10,11... | collective-permute-start | bytes 196616 | tf_op jit(solution)/shard_map/ppermute | solution.py:438
  37.6 5.8 %collective-permute-start.1 = (f32[2,32,128]{2,1,0:T(8,128)S(1)}, f32[2,32,128]{2,1,0:T(8,128)S(1)}, u32[]{:S(2)}, u32[]{:S(2)}) collective-permute-start(f32[2,32,128]{2,1,0:T(8,128)S(1)} %fusion.1), channel_id=1, source_target_pairs={{0,4},{1,5},{2,6},{3,7},{4,0},{5,1},{6,2},{7,3},{8,12},{9,13},{10,... | collective-permute-start | bytes 98312 | tf_op jit(solution)/shard_map/ppermute | solution.py:450
  43.4 6.5 %collective-permute-start.2 = (f32[2,32,128]{2,1,0:T(8,128)S(1)}, f32[2,32,128]{2,1,0:T(8,128)S(1)}, u32[]{:S(2)}, u32[]{:S(2)}) collective-permute-start(f32[2,32,128]{2,1,0:T(8,128)S(1)} %fusion.2), channel_id=1, source_target_pairs={{0,12},{1,13},{2,14},{3,15},{4,8},{5,9},{6,10},{7,11},{8,4},{9,5},... | collective-permute-start | bytes 98312 | tf_op jit(solution)/shard_map/ppermute | solution.py:450

commit v6 on v5

--- a/solution.py
+++ b/solution.py
@@ -92,13 +92,11 @@
 
 
 def prepare_kernel(
-    source_ref, shifts_ref, even_ref, odd_ref, out_ref, even_out_ref, odd_out_ref, decay_ref, gain_ref, link_ref, lead_ref, mix_ref, near_ref, end_ref,
+    source_ref, shifts_ref, even_ref, odd_ref, out_ref, even_out_ref, odd_out_ref, decay_ref, gain_ref,
     held_ref, shift_ref, sems, extra_sems,
 ):
     cells, angles, _ = out_ref.shape
     size = decay_ref.shape[0]
-    rounds = near_ref.shape[0]
-    teams = 2**rounds
     chunks = sems.shape[0]
     rows = angles // chunks
     shift_copy = pltpu.make_async_copy(
@@ -120,8 +118,7 @@
     for copy in table_copies:
         copy.start()
 
-    core, share, team = place_in_team()
-    first = share * size
+    first = place_in_team()[1] * size
     shift_copy.wait()
     shifts = jnp.concatenate(
         [
@@ -137,6 +134,18 @@
     decay = root * root
     decay_ref[...] = decay
     gain_ref[...] = axial_scale / (4.0 * rise * cosh_half)
+    for chunk, copy in enumerate(copies):
+        copy.wait()
+        swap_tiles(held_ref, out_ref, range(0, cells, min(8, cells)), range(chunk * rows, (chunk + 1) * rows, min(8, rows)))
+    for copy in table_copies:
+        copy.wait()
+
+
+def factor_kernel(cells, decay_ref, link_ref, lead_ref, mix_ref, near_ref, end_ref):
+    rounds = near_ref.shape[0]
+    teams = 2**rounds
+    core, _, team = place_in_team()
+    decay = decay_ref[...]
     one = jnp.ones_like(decay)
     zero = jnp.zeros_like(decay)
 
@@ -196,12 +205,6 @@
     end_ref[0, 1] = -to_first
     end_ref[1, 0] = -to_last
     end_ref[1, 1] = to_last * whole_decay
-
-    for chunk, copy in enumerate(copies):
-        copy.wait()
-        swap_tiles(held_ref, out_ref, range(0, cells, min(8, cells)), range(chunk * rows, (chunk + 1) * rows, min(8, rows)))
-    for copy in table_copies:
-        copy.wait()
 
 
 def place_in_team():
@@ -388,21 +391,16 @@
     ]
     rounds = swaps(teams)
 
-    turned, held_even, held_odd, decay, gain, link, lead, mix, near, ends = pl.pallas_call(
+    turned, held_even, held_odd, decay, gain = pl.pallas_call(
         prepare_kernel,
         out_shape=(
             pltpu.VMEM((depth_cells, local_t, radius_count), f32),
             *(pltpu.VMEM(table.shape, f32) for table in forward_tables),
             pltpu.VMEM((size, radius_count), f32),
             pltpu.VMEM((size, radius_count), f32),
-            pltpu.VMEM((2, merge + 1, merge, 2, size, radius_count), f32),
-            pltpu.VMEM((merge, 2, size, radius_count), f32),
-            pltpu.VMEM((len(rounds), 2, 2, size, radius_count), f32),
-            pltpu.VMEM((len(rounds), 2, size, radius_count), f32),
-            pltpu.VMEM((2, 2, size, radius_count), f32),
         ),
         in_specs=[whole(pltpu.HBM)] * 4,
-        out_specs=(whole(),) * 10,
+        out_specs=(whole(),) * 5,
         scratch_shapes=[
             pltpu.VMEM(source.shape, f32),
             pltpu.VMEM((local_t + 8, radius_count), f32),
@@ -435,6 +433,22 @@
         name="radial_forward",
         compiler_params=compact,
     )(in_vmem(modal), in_vmem(radial_basis), radial_weights.reshape(1, radius_count), in_vmem(decay))
+    decay_then, carries = lax.optimization_barrier((decay, carries))
+    link, lead, mix, near, ends = pl.pallas_call(
+        functools.partial(factor_kernel, depth_cells),
+        out_shape=(
+            pltpu.VMEM((2, merge + 1, merge, 2, size, radius_count), f32),
+            pltpu.VMEM((merge, 2, size, radius_count), f32),
+            pltpu.VMEM((len(rounds), 2, 2, size, radius_count), f32),
+            pltpu.VMEM((len(rounds), 2, size, radius_count), f32),
+            pltpu.VMEM((2, 2, size, radius_count), f32),
+        ),
+        in_specs=[whole()],
+        out_specs=(whole(),) * 5,
+        name="carry_factors",
+        compiler_params=compact,
+        cost_estimate=pl.CostEstimate(flops=1_000_000, bytes_accessed=700_000, transcendentals=0),
+    )(in_vmem(decay_then))
     twin = lax.ppermute(carries, "ax", [(index, index ^ 1) for index in range(blocks)])
     sent = (link[0, merge] * carries + link[1, merge] * twin).sum(axis=0)
     others = []

time: 80.5 us -> 80.5 us (level)
  no operation moved by 1% of the time
where the time goes in v6:
time: 80.5 us; the launch traced here: 80.3 us
  blocking collectives  60.7 us (75%)
  starting transfers between devices  8.07 us (10%)
  Pallas kernels  5.9 us (7%)
  waiting for transfers between devices  5.49 us (7%)
    all_to_all x1, blocking collectives, body(): piece = lax.all_to_all(turned, 'plane', 0, 0, tiled=True)  17.4 us
    all_to_all x1, blocking collectives, body(): lax.all_to_all(spectral, ('plane', 'ax'), 0, 0, tiled=True, axis_index_gr...  15.3 us
    all_to_all x1, blocking collectives, body(): lax.all_to_all(radial_field, ('plane', 'ax'), 0, 0, tiled=True, axis_inde...  14.4 us
    all_to_all x1, blocking collectives, body(): lax.all_to_all(spatial.reshape(planes, local_t, radius_count), 'plane', 0...  13.6 us
    ppermute x2, starting transfers between devices, body(): others.append(lax.ppermute(sent, 'ax', pairs))  7.97 us
    ppermute x2, waiting for transfers between devices, body(): others.append(lax.ppermute(sent, 'ax', pairs))  4.31 us
    pallas_call x1, Pallas kernels, body(): pl.pallas_call(prepare_kernel, out_shape=(pltpu.VMEM((depth_cells, local_...  1.75 us
  transfers between devices with their start and end apart: 3, of which 3 were waited for; matrix products, arithmetic and copies ran while one was open for 0% of the time, Pallas kernels for 0%

profile of v6, /device:TPU:8, one launch (start us, length us, event | category | flops | bytes accessed | tf_op | source)
XLA Modules:
  0.0 80.3 jit_solution(3880142307303365830)
XLA Ops:
  0.0 0.0 copy-start
  0.0 0.0 copy-start.3
  0.0 1.8 %cells_first.1 = (f32[16,64,128]{2,1,0:T(8,128)S(1)}, f32[2,256,256]{2,1,0:T(8,128)S(1)}, f32[1,512,512]{2,1,0:T(8,128)S(1)}, f32[32,128]{1,0:T(8,128)S(1)}, f32[32,128]{1,0:T(8,128)S(1)}) custom-call(f32[64,16,128]{2,1,0:T(8,128)} %source_ref.1, f32[64,128]{1,0:T(8,128)} %shifts_ref.1, f32[2,256,256]{2,1,0:T(8,128)} %constant.10.clone.even_ref, ...), custom_call_target="tpu_custom_call" | custom-call | tf_op jit(solution)/shard_map/cells_first/pallas_call | solution.py:394
  1.8 17.4 %all_to_all.20 = f32[16,64,128]{2,1,0:T(8,128)S(1)} all-to-all(f32[16,64,128]{2,1,0:T(8,128)S(1)} %get-tuple-element.21), channel_id=1, replica_groups=mesh['plane'=16,'ax'=16] {'plane'}, dimensions={0} | all-to-all | bytes 1048576 | tf_op jit(solution)/shard_map/all_to_all | solution.py:413
  19.2 0.8 %fourier_forward.1 = f32[32,32,128]{2,1,0:T(8,128)S(1)} custom-call(f32[2,256,256]{2,1,0:T(8,128)S(1)} %get-tuple-element.19.even_ref, f32[1,512,512]{2,1,0:T(8,128)S(1)} %get-tuple-element.20.odd_ref, f32[1024,128]{1,0:T(8,128)S(1)} %bitcast.21), custom_call_target="tpu_custom_call" | custom-call | tf_op jit(solution)/shard_map/fourier_forward/pallas_call | solution.py:414
  20.0 15.3 %all_to_all.21.x_ref = f32[32,32,128]{2,1,0:T(8,128)S(1)} all-to-all(f32[32,32,128]{2,1,0:T(8,128)S(1)} %fourier_forward.1), channel_id=1, replica_groups={{0,16,32,48,64,80,96,112,128,144,160,176,192,208,224,240,2,18,34,50,66,..., dimensions={0} | all-to-all | bytes 1048576 | tf_op jit(solution)/shard_map/all_to_all | solution.py:422
  35.3 0.0 copy-done
  35.3 0.0 copy-done.3
  35.3 0.9 %radial_forward.1 = (f32[32,32,128]{2,1,0:T(8,128)S(1)}, f32[2,2,32,128]{3,2,1,0:T(8,128)S(1)}) custom-call(f32[32,32,128]{2,1,0:T(8,128)S(1)} %all_to_all.21.x_ref, f32[64,128,128]{2,1,0:T(8,128)S(1)} %copy-done, f32[1,128]{1,0:T(1,128)S(1)} %bitcast.23, f32[32,128]{1,0:T(8,128)S(1)} %get-tuple-element.26.decay_ref), custom_call_target="tpu_custom_call" | custom-call | tf_op jit(solution)/shard_map/radial_forward/pallas_call | solution.py:425
  36.2 0.0 copy-start.1
  36.2 0.0 copy-start.2
  36.2 0.1 collective-permute-start
  36.3 0.1 carry_factors.1
  36.4 1.2 %collective-permute-done.twin_ref = f32[2,2,32,128]{3,2,1,0:T(8,128)S(1)} collective-permute-done((f32[2,2,32,128]{3,2,1,0:T(8,128)S(1)}, f32[2,2,32,128]{3,2,1,0:T(8,128)S(1)}, u32[]{:S(2)}, u32[]{:S(2)}) %collective-permute-start) | collective-permute-done | bytes 65568 | tf_op jit(solution)/shard_map/ppermute | solution.py:452
  37.6 3.4 %collective-permute-start.1 = (f32[2,32,128]{2,1,0:T(8,128)S(1)}, f32[2,32,128]{2,1,0:T(8,128)S(1)}, u32[]{:S(2)}, u32[]{:S(2)}) collective-permute-start(f32[2,32,128]{2,1,0:T(8,128)S(1)} %fusion.1), channel_id=1, source_target_pairs={{0,4},{1,5},{2,6},{3,7},{4,0},{5,1},{6,2},{7,3},{8,12},{9,13},{10,... | collective-permute-start | bytes 98312 | tf_op jit(solution)/shard_map/ppermute | solution.py:464
  40.9 2.4 %collective-permute-done.1.refs_0_ = f32[2,32,128]{2,1,0:T(8,128)S(1)} collective-permute-done((f32[2,32,128]{2,1,0:T(8,128)S(1)}, f32[2,32,128]{2,1,0:T(8,128)S(1)}, u32[]{:S(2)}, u32[]{:S(2)}) %collective-permute-start.1) | collective-permute-done | bytes 32800 | tf_op jit(solution)/shard_map/ppermute | solution.py:464
  43.4 4.6 %collective-permute-start.2 = (f32[2,32,128]{2,1,0:T(8,128)S(1)}, f32[2,32,128]{2,1,0:T(8,128)S(1)}, u32[]{:S(2)}, u32[]{:S(2)}) collective-permute-start(f32[2,32,128]{2,1,0:T(8,128)S(1)} %fusion.2), channel_id=1, source_target_pairs={{0,12},{1,13},{2,14},{3,15},{4,8},{5,9},{6,10},{7,11},{8,4},{9,5},... | collective-permute-start | bytes 98312 | tf_op jit(solution)/shard_map/ppermute | solution.py:464
  48.0 1.9 %collective-permute-done.2.refs_1_ = f32[2,32,128]{2,1,0:T(8,128)S(1)} collective-permute-done((f32[2,32,128]{2,1,0:T(8,128)S(1)}, f32[2,32,128]{2,1,0:T(8,128)S(1)}, u32[]{:S(2)}, u32[]{:S(2)}) %collective-permute-start.2) | collective-permute-done | bytes 32800 | tf_op jit(solution)/shard_map/ppermute | solution.py:464
  49.9 1.0 %solve_and_radial_back.1 = f32[32,32,128]{2,1,0:T(8,128)S(1)} custom-call(f32[32,32,128]{2,1,0:T(8,128)S(1)} %get-tuple-element.23.f_ref, f32[64,128,128]{2,1,0:T(8,128)S(1)} %copy-done, f32[32,128]{1,0:T(8,128)S(1)} %get-tuple-element.26.decay_ref, f32[32,128]{1,0:T(8,128)S(1)} %get-tuple-element.24.gain_ref, ...), custom_call_target="tpu_custom_call" | custom-call | tf_op jit(solution)/shard_map/solve_and_radial_back/pallas_call | solution.py:465
  50.9 14.4 %all_to_all.22.x_ref = f32[32,32,128]{2,1,0:T(8,128)S(1)} all-to-all(f32[32,32,128]{2,1,0:T(8,128)S(1)} %solve_and_radial_back.1), channel_id=1, replica_groups={{0,16,32,48,64,80,96,112,128,144,160,176,192,208,224,240,2,18,34,50,66,..., dimensions={0} | all-to-all | bytes 1048576 | tf_op jit(solution)/shard_map/all_to_all | solution.py:487
  65.3 0.0 copy-done.1
  65.3 0.0 copy-done.2
  65.3 0.6 fourier_backward.1
  65.8 13.6 %all_to_all.23.x_ref = f32[16,64,128]{2,1,0:T(8,128)S(1)} all-to-all(f32[16,64,128]{2,1,0:T(8,128)S(1)} %bitcast.22), channel_id=1, replica_groups=mesh['plane'=16,'ax'=16] {'plane'}, dimensions={0} | all-to-all | bytes 1048576 | tf_op jit(solution)/shard_map/all_to_all | solution.py:498
  79.5 0.8 %angles_first.1 = f32[64,16,128]{2,1,0:T(8,128)} custom-call(f32[16,64,128]{2,1,0:T(8,128)S(1)} %all_to_all.23.x_ref), custom_call_target="tpu_custom_call" | custom-call | tf_op jit(solution)/shard_map/angles_first/pallas_call | solution.py:501
  (2 shorter events, 0.0 us)
Async XLA Ops:
  0.0 35.3 %copy-start = (f32[64,128,128]{2,1,0:T(8,128)S(1)}, f32[64,128,128]{2,1,0:T(8,128)}, u32[]{:S(2)}) copy-start(f32[64,128,128]{2,1,0:T(8,128)} %basis_ref.3) | copy-start | bytes 12582916
  0.0 35.3 %copy-start.3 = (f32[128]{0:T(128)S(1)}, f32[128]{0:T(128)}, u32[]{:S(2)}) copy-start(f32[128]{0:T(128)} %param.10) | copy-start | bytes 1540
  36.2 29.1 %copy-start.1 = (f32[1,512,512]{2,1,0:T(8,128)S(1)}, f32[1,512,512]{2,1,0:T(8,128)}, u32[]{:S(2)}) copy-start(f32[1,512,512]{2,1,0:T(8,128)} %constant.13.clone.odd_ref) | copy-start | bytes 3145732
  36.2 29.1 %copy-start.2 = (f32[2,256,256]{2,1,0:T(8,128)S(1)}, f32[2,256,256]{2,1,0:T(8,128)}, u32[]{:S(2)}) copy-start(f32[2,256,256]{2,1,0:T(8,128)} %constant.12.clone.even_ref) | copy-start | bytes 1572868
  36.2 1.3 %collective-permute-start = (f32[2,2,32,128]{3,2,1,0:T(8,128)S(1)}, f32[2,2,32,128]{3,2,1,0:T(8,128)S(1)}, u32[]{:S(2)}, u32[]{:S(2)}) collective-permute-start(f32[2,2,32,128]{3,2,1,0:T(8,128)S(1)} %get-tuple-element.32.carry_ref), channel_id=1, source_target_pairs={{0,1},{1,0},{2,3},{3,2},{4,5},{5,4},{6,7},{7,6},{8,9},{9,8},{10,11... | collective-permute-start | bytes 196616 | tf_op jit(solution)/shard_map/ppermute | solution.py:452
  37.6 5.8 %collective-permute-start.1 = (f32[2,32,128]{2,1,0:T(8,128)S(1)}, f32[2,32,128]{2,1,0:T(8,128)S(1)}, u32[]{:S(2)}, u32[]{:S(2)}) collective-permute-start(f32[2,32,128]{2,1,0:T(8,128)S(1)} %fusion.1), channel_id=1, source_target_pairs={{0,4},{1,5},{2,6},{3,7},{4,0},{5,1},{6,2},{7,3},{8,12},{9,13},{10,... | collective-permute-start | bytes 98312 | tf_op jit(solution)/shard_map/ppermute | solution.py:464
  43.4 6.5 %collective-permute-start.2 = (f32[2,32,128]{2,1,0:T(8,128)S(1)}, f32[2,32,128]{2,1,0:T(8,128)S(1)}, u32[]{:S(2)}, u32[]{:S(2)}) collective-permute-start(f32[2,32,128]{2,1,0:T(8,128)S(1)} %fusion.2), channel_id=1, source_target_pairs={{0,12},{1,13},{2,14},{3,15},{4,8},{5,9},{6,10},{7,11},{8,4},{9,5},... | collective-permute-start | bytes 98312 | tf_op jit(solution)/shard_map/ppermute | solution.py:464

commit v7 on v6

--- a/solution.py
+++ b/solution.py
@@ -275,11 +275,16 @@
     for group in range(0, size, tile):
         rows = jnp.swapaxes(x_ref[:, group : group + tile, :] * weights, 0, 1)
         results = []
-        for inner in range(tile):
-            values = jnp.concatenate(split3(rows[inner]), axis=0)
-            basis = jnp.concatenate(split2(basis_ref[first + mode_offset(group + inner, size)]), axis=0)
-            result = mul(twice(values, 1), basis)
-            results.append(result[:depth] + (result[depth : 2 * depth] + result[2 * depth :]))
+        width = rows.shape[2]
+        for inner in range(0, tile, 2):
+            values = jnp.concatenate(split3(rows[inner]) + split3(rows[inner + 1]), axis=0)
+            pair = [
+                jnp.concatenate(split2(basis_ref[first + mode_offset(group + which, size)]), axis=0)
+                for which in (inner, inner + 1)
+            ]
+            both = mul(twice(values, 1), jnp.concatenate(pair, axis=1))
+            for half in (both[: 3 * depth, :width], both[3 * depth :, width:]):
+                results.append(half[:depth] + (half[depth : 2 * depth] + half[2 * depth :]))
         f_ref[:, group : group + tile, :] = jnp.swapaxes(jnp.stack(results), 0, 1)
     decay = decay_ref[...]
     part = depth // merge
@@ -335,11 +340,16 @@
         part = slice(group, group + tile)
         rows = jnp.swapaxes((up_ref[:, part, :] + down_ref[:, part, :]) * gain_ref[part, :], 0, 1)
         results = []
-        for inner in range(tile):
-            values = jnp.concatenate(split2(rows[inner]), axis=0)
-            basis = jnp.concatenate(split2(basis_ref[first + mode_offset(group + inner, size)]), axis=1)
-            result = mul_t(twice(values, 1), basis)
-            results.append(result[:depth] + result[depth:])
+        width = rows.shape[2]
+        for inner in range(0, tile, 2):
+            values = jnp.concatenate(split2(rows[inner]) + split2(rows[inner + 1]), axis=0)
+            pair = [
+                jnp.concatenate(split2(basis_ref[first + mode_offset(group + which, size)]), axis=1)
+                for which in (inner, inner + 1)
+            ]
+            both = mul_t(twice(values, 1), jnp.concatenate(pair, axis=0))
+            for half in (both[: 2 * depth, :width], both[2 * depth :, width:]):
+                results.append(half[:depth] + half[depth:])
         out_ref[:, part, :] = jnp.swapaxes(jnp.stack(results), 0, 1)
 
 

time: 80.5 us -> 80.4 us (level)
  no operation moved by 1% of the time
where the time goes in v7:
time: 80.4 us; the launch traced here: 80.2 us
  blocking collectives  60.7 us (75%)
  starting transfers between devices  8.07 us (10%)
  Pallas kernels  5.78 us (7%)
  waiting for transfers between devices  5.49 us (7%)
    all_to_all x1, blocking collectives, body(): piece = lax.all_to_all(turned, 'plane', 0, 0, tiled=True)  17.4 us
    all_to_all x1, blocking collectives, body(): lax.all_to_all(spectral, ('plane', 'ax'), 0, 0, tiled=True, axis_index_gr...  15.3 us
    all_to_all x1, blocking collectives, body(): lax.all_to_all(radial_field, ('plane', 'ax'), 0, 0, tiled=True, axis_inde...  14.4 us
    all_to_all x1, blocking collectives, body(): lax.all_to_all(spatial.reshape(planes, local_t, radius_count), 'plane', 0...  13.6 us
    ppermute x2, starting transfers between devices, body(): others.append(lax.ppermute(sent, 'ax', pairs))  7.97 us
    ppermute x2, waiting for transfers between devices, body(): others.append(lax.ppermute(sent, 'ax', pairs))  4.31 us
    pallas_call x1, Pallas kernels, body(): pl.pallas_call(prepare_kernel, out_shape=(pltpu.VMEM((depth_cells, local_...  1.75 us
  transfers between devices with their start and end apart: 3, of which 3 were waited for; matrix products, arithmetic and copies ran while one was open for 0% of the time, Pallas kernels for 0%

profile of v7, /device:TPU:8, one launch (start us, length us, event | category | flops | bytes accessed | tf_op | source)
XLA Modules:
  0.0 80.2 jit_solution(7417309276079054536)
XLA Ops:
  0.0 0.0 copy-start
  0.0 0.0 copy-start.3
  0.0 1.8 %cells_first.1 = (f32[16,64,128]{2,1,0:T(8,128)S(1)}, f32[2,256,256]{2,1,0:T(8,128)S(1)}, f32[1,512,512]{2,1,0:T(8,128)S(1)}, f32[32,128]{1,0:T(8,128)S(1)}, f32[32,128]{1,0:T(8,128)S(1)}) custom-call(f32[64,16,128]{2,1,0:T(8,128)} %source_ref.1, f32[64,128]{1,0:T(8,128)} %shifts_ref.1, f32[2,256,256]{2,1,0:T(8,128)} %constant.10.clone.even_ref, ...), custom_call_target="tpu_custom_call" | custom-call | tf_op jit(solution)/shard_map/cells_first/pallas_call | solution.py:404
  1.8 17.4 %all_to_all.20 = f32[16,64,128]{2,1,0:T(8,128)S(1)} all-to-all(f32[16,64,128]{2,1,0:T(8,128)S(1)} %get-tuple-element.21), channel_id=1, replica_groups=mesh['plane'=16,'ax'=16] {'plane'}, dimensions={0} | all-to-all | bytes 1048576 | tf_op jit(solution)/shard_map/all_to_all | solution.py:423
  19.2 0.8 %fourier_forward.1 = f32[32,32,128]{2,1,0:T(8,128)S(1)} custom-call(f32[2,256,256]{2,1,0:T(8,128)S(1)} %get-tuple-element.19.even_ref, f32[1,512,512]{2,1,0:T(8,128)S(1)} %get-tuple-element.20.odd_ref, f32[1024,128]{1,0:T(8,128)S(1)} %bitcast.21), custom_call_target="tpu_custom_call" | custom-call | tf_op jit(solution)/shard_map/fourier_forward/pallas_call | solution.py:424
  20.0 15.3 %all_to_all.21.x_ref = f32[32,32,128]{2,1,0:T(8,128)S(1)} all-to-all(f32[32,32,128]{2,1,0:T(8,128)S(1)} %fourier_forward.1), channel_id=1, replica_groups={{0,16,32,48,64,80,96,112,128,144,160,176,192,208,224,240,2,18,34,50,66,..., dimensions={0} | all-to-all | bytes 1048576 | tf_op jit(solution)/shard_map/all_to_all | solution.py:432
  35.3 0.0 copy-done
  35.3 0.0 copy-done.3
  35.3 0.8 %radial_forward.1 = (f32[32,32,128]{2,1,0:T(8,128)S(1)}, f32[2,2,32,128]{3,2,1,0:T(8,128)S(1)}) custom-call(f32[32,32,128]{2,1,0:T(8,128)S(1)} %all_to_all.21.x_ref, f32[64,128,128]{2,1,0:T(8,128)S(1)} %copy-done, f32[1,128]{1,0:T(1,128)S(1)} %bitcast.23, f32[32,128]{1,0:T(8,128)S(1)} %get-tuple-element.26.decay_ref), custom_call_target="tpu_custom_call" | custom-call | tf_op jit(solution)/shard_map/radial_forward/pallas_call | solution.py:435
  36.1 0.0 copy-start.1
  36.1 0.0 copy-start.2
  36.2 0.1 collective-permute-start
  36.3 0.1 carry_factors.1
  36.3 1.2 %collective-permute-done.twin_ref = f32[2,2,32,128]{3,2,1,0:T(8,128)S(1)} collective-permute-done((f32[2,2,32,128]{3,2,1,0:T(8,128)S(1)}, f32[2,2,32,128]{3,2,1,0:T(8,128)S(1)}, u32[]{:S(2)}, u32[]{:S(2)}) %collective-permute-start) | collective-permute-done | bytes 65568 | tf_op jit(solution)/shard_map/ppermute | solution.py:462
  37.5 3.4 %collective-permute-start.1 = (f32[2,32,128]{2,1,0:T(8,128)S(1)}, f32[2,32,128]{2,1,0:T(8,128)S(1)}, u32[]{:S(2)}, u32[]{:S(2)}) collective-permute-start(f32[2,32,128]{2,1,0:T(8,128)S(1)} %fusion.1), channel_id=1, source_target_pairs={{0,4},{1,5},{2,6},{3,7},{4,0},{5,1},{6,2},{7,3},{8,12},{9,13},{10,... | collective-permute-start | bytes 98312 | tf_op jit(solution)/shard_map/ppermute | solution.py:474
  40.9 2.4 %collective-permute-done.1.refs_0_ = f32[2,32,128]{2,1,0:T(8,128)S(1)} collective-permute-done((f32[2,32,128]{2,1,0:T(8,128)S(1)}, f32[2,32,128]{2,1,0:T(8,128)S(1)}, u32[]{:S(2)}, u32[]{:S(2)}) %collective-permute-start.1) | collective-permute-done | bytes 32800 | tf_op jit(solution)/shard_map/ppermute | solution.py:474
  43.3 4.6 %collective-permute-start.2 = (f32[2,32,128]{2,1,0:T(8,128)S(1)}, f32[2,32,128]{2,1,0:T(8,128)S(1)}, u32[]{:S(2)}, u32[]{:S(2)}) collective-permute-start(f32[2,32,128]{2,1,0:T(8,128)S(1)} %fusion.2), channel_id=1, source_target_pairs={{0,12},{1,13},{2,14},{3,15},{4,8},{5,9},{6,10},{7,11},{8,4},{9,5},... | collective-permute-start | bytes 98312 | tf_op jit(solution)/shard_map/ppermute | solution.py:474
  47.9 1.9 %collective-permute-done.2.refs_1_ = f32[2,32,128]{2,1,0:T(8,128)S(1)} collective-permute-done((f32[2,32,128]{2,1,0:T(8,128)S(1)}, f32[2,32,128]{2,1,0:T(8,128)S(1)}, u32[]{:S(2)}, u32[]{:S(2)}) %collective-permute-start.2) | collective-permute-done | bytes 32800 | tf_op jit(solution)/shard_map/ppermute | solution.py:474
  49.8 0.9 %solve_and_radial_back.1 = f32[32,32,128]{2,1,0:T(8,128)S(1)} custom-call(f32[32,32,128]{2,1,0:T(8,128)S(1)} %get-tuple-element.23.f_ref, f32[64,128,128]{2,1,0:T(8,128)S(1)} %copy-done, f32[32,128]{1,0:T(8,128)S(1)} %get-tuple-element.26.decay_ref, f32[32,128]{1,0:T(8,128)S(1)} %get-tuple-element.24.gain_ref, ...), custom_call_target="tpu_custom_call" | custom-call | tf_op jit(solution)/shard_map/solve_and_radial_back/pallas_call | solution.py:475
  50.8 14.4 %all_to_all.22.x_ref = f32[32,32,128]{2,1,0:T(8,128)S(1)} all-to-all(f32[32,32,128]{2,1,0:T(8,128)S(1)} %solve_and_radial_back.1), channel_id=1, replica_groups={{0,16,32,48,64,80,96,112,128,144,160,176,192,208,224,240,2,18,34,50,66,..., dimensions={0} | all-to-all | bytes 1048576 | tf_op jit(solution)/shard_map/all_to_all | solution.py:497
  65.2 0.0 copy-done.1
  65.2 0.0 copy-done.2
  65.2 0.6 fourier_backward.1
  65.7 13.6 %all_to_all.23.x_ref = f32[16,64,128]{2,1,0:T(8,128)S(1)} all-to-all(f32[16,64,128]{2,1,0:T(8,128)S(1)} %bitcast.22), channel_id=1, replica_groups=mesh['plane'=16,'ax'=16] {'plane'}, dimensions={0} | all-to-all | bytes 1048576 | tf_op jit(solution)/shard_map/all_to_all | solution.py:508
  79.4 0.8 %angles_first.1 = f32[64,16,128]{2,1,0:T(8,128)} custom-call(f32[16,64,128]{2,1,0:T(8,128)S(1)} %all_to_all.23.x_ref), custom_call_target="tpu_custom_call" | custom-call | tf_op jit(solution)/shard_map/angles_first/pallas_call | solution.py:511
  (2 shorter events, 0.0 us)
Async XLA Ops:
  0.0 35.3 %copy-start = (f32[64,128,128]{2,1,0:T(8,128)S(1)}, f32[64,128,128]{2,1,0:T(8,128)}, u32[]{:S(2)}) copy-start(f32[64,128,128]{2,1,0:T(8,128)} %basis_ref.3) | copy-start | bytes 12582916
  0.0 35.3 %copy-start.3 = (f32[128]{0:T(128)S(1)}, f32[128]{0:T(128)}, u32[]{:S(2)}) copy-start(f32[128]{0:T(128)} %param.10) | copy-start | bytes 1540
  36.1 29.0 %copy-start.1 = (f32[1,512,512]{2,1,0:T(8,128)S(1)}, f32[1,512,512]{2,1,0:T(8,128)}, u32[]{:S(2)}) copy-start(f32[1,512,512]{2,1,0:T(8,128)} %constant.13.clone.odd_ref) | copy-start | bytes 3145732
  36.1 29.0 %copy-start.2 = (f32[2,256,256]{2,1,0:T(8,128)S(1)}, f32[2,256,256]{2,1,0:T(8,128)}, u32[]{:S(2)}) copy-start(f32[2,256,256]{2,1,0:T(8,128)} %constant.12.clone.even_ref) | copy-start | bytes 1572868
  36.2 1.3 %collective-permute-start = (f32[2,2,32,128]{3,2,1,0:T(8,128)S(1)}, f32[2,2,32,128]{3,2,1,0:T(8,128)S(1)}, u32[]{:S(2)}, u32[]{:S(2)}) collective-permute-start(f32[2,2,32,128]{3,2,1,0:T(8,128)S(1)} %get-tuple-element.32.carry_ref), channel_id=1, source_target_pairs={{0,1},{1,0},{2,3},{3,2},{4,5},{5,4},{6,7},{7,6},{8,9},{9,8},{10,11... | collective-permute-start | bytes 196616 | tf_op jit(solution)/shard_map/ppermute | solution.py:462
  37.5 5.8 %collective-permute-start.1 = (f32[2,32,128]{2,1,0:T(8,128)S(1)}, f32[2,32,128]{2,1,0:T(8,128)S(1)}, u32[]{:S(2)}, u32[]{:S(2)}) collective-permute-start(f32[2,32,128]{2,1,0:T(8,128)S(1)} %fusion.1), channel_id=1, source_target_pairs={{0,4},{1,5},{2,6},{3,7},{4,0},{5,1},{6,2},{7,3},{8,12},{9,13},{10,... | collective-permute-start | bytes 98312 | tf_op jit(solution)/shard_map/ppermute | solution.py:474
  43.3 6.5 %collective-permute-start.2 = (f32[2,32,128]{2,1,0:T(8,128)S(1)}, f32[2,32,128]{2,1,0:T(8,128)S(1)}, u32[]{:S(2)}, u32[]{:S(2)}) collective-permute-start(f32[2,32,128]{2,1,0:T(8,128)S(1)} %fusion.2), channel_id=1, source_target_pairs={{0,12},{1,13},{2,14},{3,15},{4,8},{5,9},{6,10},{7,11},{8,4},{9,5},... | collective-permute-start | bytes 98312 | tf_op jit(solution)/shard_map/ppermute | solution.py:474
